TPU v7x, 128 devices: a whole 4x4x4 slice. The times are simulated.
128 devices in a mesh: dp: 8 (over x, y_hi), head: 16 (over y_lo, z, core).
Axes of the slice: x: 4, y: 4 (y_hi: 2, y_lo: 2; y = y_hi * 2 + y_lo), z: 4, core: 2. Of those that a mesh axis runs over, the one named last changes fastest.
Arguments:
- inputs: bfloat16 [2048, 8192], P(('dp', 'head')), may hold values from -6 to 6
- gain: float32 [8192], replicated, may hold values from 0.1 to 1.9
- doc_ids: int32 [8, 256], P('dp'), may hold values from 0 to 3, never falling along the last dimension, each value on 1 to 128 neighbouring positions
- w_query: bfloat16 [8192, 8192], P(None, 'head'), may hold values from -0.0625 to 0.0625
- w_key: bfloat16 [8192, 1024], P(None, 'head'), may hold values from -0.0625 to 0.0625
- w_value: bfloat16 [8192, 1024], P(None, 'head'), may hold values from -0.0625 to 0.0625
- w_out: bfloat16 [8192, 8192], P('head'), may hold values from -0.0625 to 0.0625
- grad_out: bfloat16 [2048, 8192], P(('dp', 'head')), may hold values from -6 to 6
Outputs:
- outputs: bfloat16 [2048, 8192], P(('dp', 'head'))
- grad_in: bfloat16 [2048, 8192], P(('dp', 'head'))
- grad_gain: float32 [8192], replicated
- grad_wq: bfloat16 [8192, 8192], P('dp', 'head')
- grad_wk: bfloat16 [8192, 1024], P('dp', 'head')
- grad_wv: bfloat16 [8192, 1024], P('dp', 'head')
- grad_wo: bfloat16 [8192, 8192], P('head', 'dp')
Inputs may be any that keep to these rules, and one draw needn't show every extreme that they name: `doc_ids`: document numbers never fall along a sequence; every document holds 1 to 128 tokens and one holds exactly 128.
All inputs are finite; a program needn't handle non-finite values.
Results may differ from a plain program's by a relative error of at most 0.03.
Values may be sent and summed in bfloat16 or wider, within the bound.
A program may use at most 128 MiB of HBM per device.

v0:
```python
import jax
import jax.numpy as jnp
from jax import lax
from jax.sharding import PartitionSpec as P

EPSILON = 1e-05
THETA = 500000.0


def from_partner(x, axis, bit):
    return lax.ppermute(x, axis, [(i, i ^ 1 << bit) for i in range(lax.axis_size(axis))])


def rotate(values):
    half_dim = values.shape[-1] // 2
    return jnp.concatenate([-values[..., half_dim:], values[..., :half_dim]], axis=-1)


def rotate_back(values):
    half_dim = values.shape[-1] // 2
    return jnp.concatenate([values[..., half_dim:], -values[..., :half_dim]], axis=-1)


def tables(documents, head_dim):
    length = documents.shape[0]
    indices = jnp.arange(length, dtype=jnp.int32)
    starts = jnp.concatenate([jnp.ones((1,), dtype=bool), documents[1:] != documents[:-1]])
    first_index = lax.cummax(jnp.where(starts, indices, 0), axis=0)
    position = (indices - first_index).astype(jnp.float32)
    exponent = jnp.arange(head_dim // 2, dtype=jnp.float32) * (2.0 / head_dim)
    frequency = THETA ** (-exponent)
    angles = position[:, None] * frequency[None, :]
    cosine_table = jnp.concatenate([jnp.cos(angles)] * 2, axis=-1)
    sine_table = jnp.concatenate([jnp.sin(angles)] * 2, axis=-1)
    allowed = (documents[:, None] == documents[None, :]) & (indices[:, None] >= indices[None, :])
    return (cosine_table, sine_table, allowed)


def over_rows(left, right):
    return lax.dot_general(
        left, right, (((0,), (0,)), ((), ())), preferred_element_type=jnp.float32
    )


def per_device(inputs, gain, doc_ids, w_query, w_key, w_value, w_out, grad_out):
    local_rows, model_width = inputs.shape
    head_count = lax.axis_size("head")
    seq_len = local_rows * head_count
    half_dim = w_key.shape[1]
    head_dim = 2 * half_dim
    group_heads = w_query.shape[1] // head_dim
    score_scale = head_dim ** (-0.5)
    pair_side = lax.axis_index("head") % 2
    cosine_table, sine_table, allowed = tables(doc_ids[0], head_dim)
    cosine_wide = cosine_table[:, None, :]
    sine_wide = sine_table[:, None, :]
    input_wide = inputs.astype(jnp.float32)
    inverse_rms = lax.rsqrt(jnp.mean(input_wide * input_wide, axis=-1, keepdims=True) + EPSILON)
    normed = (input_wide * inverse_rms * gain).astype(jnp.bfloat16)
    normed_all = lax.all_gather(normed, "head", axis=0, tiled=True)
    query_pre = jnp.dot(normed_all, w_query, preferred_element_type=jnp.float32).astype(
        jnp.bfloat16
    )
    own_weights = jnp.stack([w_key, w_value])
    other_weights = from_partner(own_weights, "head", 0)
    joined = jnp.where(
        pair_side == 0,
        jnp.concatenate([own_weights, other_weights], axis=2),
        jnp.concatenate([other_weights, own_weights], axis=2),
    )
    key_pre = jnp.dot(normed_all, joined[0], preferred_element_type=jnp.float32).astype(
        jnp.bfloat16
    )
    values = jnp.dot(normed_all, joined[1], preferred_element_type=jnp.float32).astype(jnp.bfloat16)
    query_wide = query_pre.astype(jnp.float32).reshape(seq_len, group_heads, head_dim)
    key_wide = key_pre.astype(jnp.float32)
    queries = (query_wide * cosine_wide + rotate(query_wide) * sine_wide).astype(jnp.bfloat16)
    key_rows = (key_wide * cosine_table + rotate(key_wide) * sine_table).astype(jnp.bfloat16)
    scores = (
        jnp.einsum("qhd,kd->hqk", queries, key_rows, preferred_element_type=jnp.float32)
        * score_scale
    )
    scores = jnp.where(allowed[None], scores, -1e30)
    attn_probs = jax.nn.softmax(scores, axis=-1)
    probs_low = attn_probs.astype(jnp.bfloat16)
    attended = jnp.einsum(
        "hqk,kd->qhd", probs_low, values, preferred_element_type=jnp.float32
    ).astype(jnp.bfloat16)
    attended = attended.reshape(seq_len, group_heads * head_dim)
    attn_sum = lax.psum_scatter(
        jnp.dot(attended, w_out, preferred_element_type=jnp.float32).astype(jnp.bfloat16),
        "head",
        scatter_dimension=0,
        tiled=True,
    ).astype(jnp.float32)
    outputs = (input_wide + attn_sum).astype(jnp.bfloat16)
    grad_all = lax.all_gather(grad_out, "head", axis=0, tiled=True)
    grad_att = jnp.dot(grad_all, w_out.T, preferred_element_type=jnp.float32).astype(jnp.bfloat16)
    grad_att = grad_att.reshape(seq_len, group_heads, head_dim)
    grad_probs = jnp.einsum("qhd,kd->hqk", grad_att, values, preferred_element_type=jnp.float32)
    row_delta = jnp.sum(attn_probs * grad_probs, axis=-1, keepdims=True)
    grad_scores = (attn_probs * (grad_probs - row_delta)).astype(jnp.bfloat16)
    grad_query = (
        jnp.einsum("hqk,kd->qhd", grad_scores, key_rows, preferred_element_type=jnp.float32)
        * score_scale
    )
    query_raw = (grad_query * cosine_wide + rotate_back(grad_query * sine_wide)).astype(
        jnp.bfloat16
    )
    query_raw = query_raw.reshape(seq_len, group_heads * head_dim)
    key_sum = (
        jnp.einsum("hqk,qhd->kd", grad_scores, queries, preferred_element_type=jnp.float32)
        * score_scale
    )
    key_group = (key_sum * cosine_table + rotate_back(key_sum * sine_table)).astype(jnp.bfloat16)
    value_group = jnp.einsum(
        "hqk,qhd->kd", probs_low, grad_att, preferred_element_type=jnp.float32
    ).astype(jnp.bfloat16)
    stacked = jnp.stack([key_group, value_group])
    own_half = jnp.where(pair_side == 0, stacked[..., :half_dim], stacked[..., half_dim:])
    give_half = jnp.where(pair_side == 0, stacked[..., half_dim:], stacked[..., :half_dim])
    received = from_partner(give_half, "head", 0)
    pair_half = (own_half.astype(jnp.float32) + received.astype(jnp.float32)).astype(jnp.bfloat16)
    part_key = pair_half[0]
    part_value = pair_half[1]
    result = jnp.dot(query_raw, w_query.T, preferred_element_type=jnp.float32)
    result = result + jnp.dot(part_key, w_key.T, preferred_element_type=jnp.float32)
    grad_normed = lax.psum_scatter(
        (result + jnp.dot(part_value, w_value.T, preferred_element_type=jnp.float32)).astype(
            jnp.bfloat16
        ),
        "head",
        scatter_dimension=0,
        tiled=True,
    ).astype(jnp.float32)
    gain_part = jnp.sum(grad_normed * input_wide * inverse_rms, axis=0)
    scaled = grad_normed * gain
    grad_in = (
        grad_out.astype(jnp.float32)
        + inverse_rms * scaled
        - input_wide * inverse_rms**3 * jnp.mean(scaled * input_wide, axis=-1, keepdims=True)
    ).astype(jnp.bfloat16)
    grad_gain = lax.psum(gain_part, ("dp", "head"))
    pair_cols = jnp.concatenate([pair_half[0], pair_half[1]], axis=1)
    normed_cols = normed_all
    grad_wq = lax.psum_scatter(
        over_rows(normed_cols, query_raw).astype(jnp.bfloat16),
        "dp",
        scatter_dimension=0,
        tiled=True,
    )
    normed_cols = normed_all
    grad_kv = lax.psum_scatter(
        over_rows(normed_cols, pair_cols).astype(jnp.bfloat16),
        "dp",
        scatter_dimension=0,
        tiled=True,
    ).astype(jnp.float32)
    grad_wk = grad_kv[:, :half_dim].astype(jnp.bfloat16)
    grad_wv = grad_kv[:, half_dim:].astype(jnp.bfloat16)
    partial_out = over_rows(attended, grad_all)
    grad_wo = lax.psum_scatter(
        partial_out.astype(jnp.bfloat16), "dp", scatter_dimension=1, tiled=True
    )
    return (outputs, grad_in, grad_gain, grad_wq, grad_wk, grad_wv, grad_wo)


def solution(mesh):
    return jax.shard_map(
        per_device,
        mesh=mesh,
        in_specs=(
            P(("dp", "head"), None),
            P(),
            P("dp", None),
            P(None, "head"),
            P(None, "head"),
            P(None, "head"),
            P("head", None),
            P(("dp", "head"), None),
        ),
        out_specs=(
            P(("dp", "head"), None),
            P(("dp", "head"), None),
            P(),
            P("dp", "head"),
            P("dp", "head"),
            P("dp", "head"),
            P("head", "dp"),
        ),
        check_vma=False,
    )
```

profile of v0, /device:TPU:1, one launch (start us, length us, event | category | flops | bytes accessed | tf_op | source)
XLA Modules:
  0.0 572.0 jit_solution(8109283809783559333)
XLA Ops:
  7.2 0.7 all-gather.5.cloned.1.call-update
  8.0 1.1 fusion.20
  9.1 1.8 fusion.22
  11.0 3.1 pad_maximum_fusion
  14.1 1.4 collective-permute-start
  15.7 0.3 reduce-window.9
  16.3 0.7 fusion.33
  17.0 0.3 multiply_cosine_fusion
  17.4 2.3 collective-permute-done
  19.6 4.5 maximum_select_fusion
  24.1 26.7 %all-gather.5.cloned.1.call-done = bf16[256,8192]{1,0:T(8,128)(2,1)} async-done(((bf16[16,8192]{1,0:T(8,128)(2,1)}), bf16[256,8192]{1,0:T(8,128)(2,1)}) %all-gather.5.cloned.1.call-update) | async-done | bytes 4194320 | tf_op jit(solution)/shard_map/all_gather | solution.py:97
  50.8 7.0 %convolution_convert_fusion.5 = bf16[256,512]{1,0:T(8,128)(2,1)S(1)} fusion(bf16[256,8192]{1,0:T(8,128)(2,1)} %all-gather.5.cloned.1.call-done, bf16[512,8192]{1,0:T(8,128)(2,1)} %param.14), kind=kOutput, calls=%fused_computation.22 | convolution fusion | flops 2147614720 | bytes 12845056 | tf_op jit(solution)/shard_map/dot_general | solution.py:98
  57.9 0.8 copy.53
  58.7 31.9 %all-gather.3.cloned.1.call-done = bf16[256,8192]{1,0:T(8,128)(2,1)} async-done(((bf16[16,8192]{1,0:T(8,128)(2,1)}), bf16[256,8192]{1,0:T(8,128)(2,1)}) %all-gather.3.cloned.1.call-update) | async-done | bytes 4194320 | tf_op jit(solution)/shard_map/all_gather | solution.py:60
  90.6 7.0 %fusion.8 = f32[256,512]{1,0:T(8,128)S(1)} fusion(bf16[256,8192]{1,0:T(8,128)(2,1)} %all-gather.3.cloned.1.call-done, bf16[8192,512]{1,0:T(8,128)(2,1)} %param.11), kind=kOutput, calls=%fused_computation.24 | convolution fusion | flops 2147745792 | bytes 13107200 | tf_op jit(solution)/shard_map/dot_general | solution.py:61
  97.8 4.4 fusion.13
  102.2 0.7 pad_maximum_fusion.1
  103.0 1.4 fusion.53
  104.4 2.8 fusion.14
  107.2 4.1 fusion.15
  111.4 0.3 multiply_reduce_fusion
  111.7 1.6 multiply_convert_fusion
  113.3 0.3 fusion.43
  113.6 0.7 fusion.38
  114.3 0.5 collective-permute-start.1
  114.8 1.0 collective-permute-done.1
  115.9 2.7 convolution_convert_fusion.3
  118.6 0.2 broadcast_multiply_fusion
  118.9 0.5 copy-done.6
  119.5 5.8 %fusion.54 = f32[256,8192]{1,0:T(8,128)S(1)} fusion(bf16[256,512]{0,1:T(8,128)(2,1)S(1)} %bitcast.116, bf16[8192,512]{1,0:T(8,128)(2,1)} %param.11), kind=kOutput, calls=%fused_computation.113 | convolution fusion | flops 2147483648 | bytes 17039360 | tf_op jit(solution)/shard_map/dot_general | solution.py:126
  125.3 1.3 convolution_add_fusion.1
  126.6 3.3 fusion.1
  130.0 0.8 copy-done.13
  130.7 1.6 convolution_convert_fusion.4
  132.3 7.8 %convolution_convert_fusion.2 = bf16[256,8192]{1,0:T(8,128)(2,1)} fusion(bf16[256,512]{0,1:T(8,128)(2,1)S(1)} %bitcast.118, bf16[512,8192]{1,0:T(8,128)(2,1)} %param.14), kind=kOutput, calls=%fused_computation.6 | convolution fusion | flops 2149580800 | bytes 12845056 | tf_op jit(solution)/shard_map/dot_general | solution.py:91
  140.1 7.9 %convolution_convert_fusion.1 = bf16[8192,512]{1,0:T(8,128)(2,1)} fusion(bf16[256,8192]{1,0:T(8,128)(2,1)} %all-gather.3.cloned.1.call-done, bf16[256,512]{0,1:T(8,128)(2,1)S(1)} %bitcast.117), kind=kOutput, calls=%fused_computation.2 | convolution fusion | flops 2151677952 | bytes 12845056 | tf_op jit(solution)/shard_map/dot_general | solution.py:40
  148.1 0.3 reduce-scatter.14.cloned.1.call-start
  148.4 7.8 %convolution_convert_fusion = bf16[512,8192]{1,0:T(8,128)(2,1)} fusion(bf16[256,512]{0,1:T(8,128)(2,1)S(1)} %bitcast.119, bf16[256,8192]{1,0:T(8,128)(2,1)} %all-gather.5.cloned.1.call-done), kind=kOutput, calls=%fused_computation.1 | convolution fusion | flops 2151677952 | bytes 12845056 | tf_op jit(solution)/shard_map/dot_general | solution.py:40
  156.2 35.9 %reduce-scatter.12.cloned.1.call-done = bf16[1024,128]{1,0:T(8,128)(2,1)} async-done(((bf16[8192,128]{1,0:T(8,128)(2,1)}), bf16[1024,128]{1,0:T(8,128)(2,1)}) %reduce-scatter.12.cloned.1.call-update) | async-done | bytes 262160 | tf_op jit(solution)/shard_map/reduce_scatter | solution.py:153
  192.1 1.2 fusion.51
  193.3 0.8 copy.42
  194.1 0.8 copy.41
  194.8 62.9 %reduce-scatter.8.cloned.1.call-done = bf16[16,8192]{1,0:T(8,128)(2,1)} async-done(((bf16[256,8192]{1,0:T(8,128)(2,1)}), bf16[16,8192]{1,0:T(8,128)(2,1)}) %reduce-scatter.8.cloned.1.call-update) | async-done | bytes 262160 | tf_op jit(solution)/shard_map/reduce_scatter | solution.py:128
  257.8 1.3 fusion.27
  259.0 69.6 %psum.7 = f32[8192]{0:T(1024)} all-reduce(f32[8192]{0:T(1024)S(1)} %get-tuple-element.21), channel_id=1, replica_groups=mesh['dp'=8,'head'=16] {'dp','head'}, use_global_device_ids=true, to_apply=%region_10.11 | all-reduce | flops 8192 | bytes 65536 | tf_op jit(solution)/shard_map/psum | solution.py:143
  328.6 2.1 fusion.19
  330.7 116.1 %reduce-scatter.10.cloned.1.call-done = bf16[1024,512]{1,0:T(8,128)(2,1)} async-done(((bf16[8192,512]{1,0:T(8,128)(2,1)}), bf16[1024,512]{1,0:T(8,128)(2,1)}) %reduce-scatter.10.cloned.1.call-update) | async-done | bytes 1048592 | tf_op jit(solution)/shard_map/reduce_scatter | solution.py:146
  446.8 118.3 %reduce-scatter.14.cloned.1.call-done = bf16[512,1024]{1,0:T(8,128)(2,1)} async-done(((bf16[512,8192]{1,0:T(8,128)(2,1)}), bf16[512,1024]{1,0:T(8,128)(2,1)}) %reduce-scatter.14.cloned.1.call-update) | async-done | bytes 1048592 | tf_op jit(solution)/shard_map/reduce_scatter | solution.py:162
  (58 shorter events, 1.4 us)
Async XLA Ops:
  7.2 12.5 %copy-start.2 = (bf16[8192,64]{0,1:T(8,128)(2,1)S(1)}, bf16[8192,64]{0,1:T(8,128)(2,1)}, u32[]{:S(2)}) copy-start(bf16[8192,64]{0,1:T(8,128)(2,1)} %param.13) | copy-start | bytes 3145732
  7.2 12.5 %copy-start.1 = (bf16[8192,64]{0,1:T(8,128)(2,1)S(1)}, bf16[8192,64]{0,1:T(8,128)(2,1)}, u32[]{:S(2)}) copy-start(bf16[8192,64]{0,1:T(8,128)(2,1)} %param.12) | copy-start | bytes 3145732
  7.2 8.3 %copy-start.11 = (s32[1,256]{1,0:T(1,128)S(1)}, s32[1,256]{1,0:T(1,128)}, u32[]{:S(2)}) copy-start(s32[1,256]{1,0:T(1,128)} %param.10) | copy-start | bytes 3076
  7.2 43.6 %all-gather.5.cloned.1.call-start = ((), (), s32[]{:S(2)}) async-start(), calls=%async_computation.7 | async-start | bytes 4456448 | tf_op jit(solution)/shard_map/all_gather | solution.py:97
  7.9 82.6 %all-gather.3.cloned.1.call-start = ((), (), s32[]{:S(2)}) async-start(), calls=%async_computation.5 | async-start | bytes 4456448 | tf_op jit(solution)/shard_map/all_gather | solution.py:60
  10.9 181.2 %reduce-scatter.12.cloned.1.call-start = ((), (), s32[]{:S(2)}) async-start(), calls=%async_computation.10 | async-start | bytes 2359296 | tf_op jit(solution)/shard_map/reduce_scatter | solution.py:153
  14.1 5.6 collective-permute-start
  104.4 7.0 %copy-start.5 = (f32[4,256,256]{1,2,0:T(8,128)}, f32[4,256,256]{1,2,0:T(8,128)S(1)}, u32[]{:S(2)}) copy-start(f32[4,256,256]{1,2,0:T(8,128)S(1)} %get-tuple-element.49) | copy-start | bytes 3145732
  107.2 4.2 copy-start.9
  111.3 3.0 copy-start.12
  111.3 2.9 copy-start.10
  111.4 4.5 copy-start
  114.3 1.5 collective-permute-start.1
  115.9 2.8 copy-start.8
  118.5 0.9 copy-start.6
  118.6 139.2 %reduce-scatter.8.cloned.1.call-start = ((), (), s32[]{:S(2)}) async-start(), calls=%async_computation.8 | async-start | bytes 4456448 | tf_op jit(solution)/shard_map/reduce_scatter | solution.py:128
  129.9 0.8 copy-start.13
  129.9 198.7 %reduce-scatter.6.cloned.1.call-start = ((), (), s32[]{:S(2)}) async-start(), calls=%async_computation.6 | async-start | bytes 4456448 | tf_op jit(solution)/shard_map/reduce_scatter | solution.py:90
  140.1 306.7 %reduce-scatter.10.cloned.1.call-start = ((), (), s32[]{:S(2)}) async-start(), calls=%async_computation.9 | async-start | bytes 9437184 | tf_op jit(solution)/shard_map/reduce_scatter | solution.py:146
  148.1 417.0 %reduce-scatter.14.cloned.1.call-start = ((), (), s32[]{:S(2)}) async-start(), calls=%async_computation.11 | async-start | bytes 9437184 | tf_op jit(solution)/shard_map/reduce_scatter | solution.py:162
  156.2 101.6 %copy-start.3 = (bf16[16,8192]{1,0:T(8,128)(2,1)S(1)}, bf16[16,8192]{1,0:T(8,128)(2,1)}, u32[]{:S(2)}) copy-start(bf16[16,8192]{1,0:T(8,128)(2,1)} %param.8) | copy-start | bytes 786436
  156.2 101.6 %copy-start.7 = (f32[8192]{0:T(1024)S(1)}, f32[8192]{0:T(1024)}, u32[]{:S(2)}) copy-start(f32[8192]{0:T(1024)} %param.9) | copy-start | bytes 98308
  156.2 172.4 %copy-start.4 = (bf16[16,8192]{1,0:T(8,128)(2,1)S(1)}, bf16[16,8192]{1,0:T(8,128)(2,1)}, u32[]{:S(2)}) copy-start(bf16[16,8192]{1,0:T(8,128)(2,1)} %param.15) | copy-start | bytes 786436
Sparse Core Ops, SparseCore 0:
  9.7 41.0 all-gather.4
  53.1 37.4 all-gather.2
  118.7 73.3 reduce-scatter.11
  194.5 63.2 reduce-scatter.7
  260.1 65.8 reduce-scatter.5
  330.8 115.9 reduce-scatter.9
  451.8 113.3 reduce-scatter.13
where the time goes:
time: 573 us; the launch traced here: 572 us
  waiting for transfers between devices  396 us (69%)
  blocking collectives  69.6 us (12%)
  matrix products  65.6 us (11%)
  other arithmetic  18.7 us (3%)
  between operations  14.4 us (3%)
    reduce_scatter x1, waiting for transfers between devices, per_device(): lax.psum_scatter(partial_out.astype(jnp.bfloat16), 'dp', scatter_dimensio...  118 us
    reduce_scatter x1, waiting for transfers between devices, per_device(): lax.psum_scatter(over_rows(normed_cols, query_raw).astype(jnp.bfloat16),...  116 us
    psum x1, blocking collectives, per_device(): grad_gain = lax.psum(gain_part, ('dp', 'head'))  69.6 us
    reduce_scatter x1, waiting for transfers between devices, per_device(): lax.psum_scatter((result + jnp.dot(part_value, w_value.T, preferred_eleme...  62.9 us
    reduce_scatter x1, waiting for transfers between devices, per_device(): lax.psum_scatter(over_rows(normed_cols, pair_cols).astype(jnp.bfloat16),...  35.9 us
    all_gather x1, waiting for transfers between devices, per_device(): normed_all = lax.all_gather(normed, 'head', axis=0, tiled=True)  31.9 us
    all_gather x1, waiting for transfers between devices, per_device(): grad_all = lax.all_gather(grad_out, 'head', axis=0, tiled=True)  26.7 us
    dot_general x3, matrix products, over_rows(): lax.dot_general(left, right, (((0,), (0,)), ((), ())), preferred_element_...  18.4 us
  transfers between devices with their start and end apart: 9, of which 8 were waited for; matrix products, arithmetic and copies ran while one was open for 11% of the time, Pallas kernels for 0%

commit v1 on v0

v1 whole, which is shorter than its diff:
```python
import functools

import jax
import jax.numpy as jnp
from jax import lax
from jax.experimental import pallas as pl
from jax.experimental.pallas import tpu as pltpu
from jax.sharding import PartitionSpec as P

EPSILON = 1e-05
THETA = 500000.0
MESH = pl.DeviceIdType.MESH
BF = jnp.bfloat16
F32 = jnp.float32

ROWS = 16
CHUNKS = 8
CHUNK = 1024
SEQ = 256
HEADS = 4
HD = 128


def device(x, yh, yl, z, c):
    return (x * 2 + yh, (yl * 4 + z) * 2 + c)


def dot(a, b):
    return jnp.dot(a, b, preferred_element_type=F32)


def dot_nt(a, b):
    return lax.dot_general(a, b, (((1,), (1,)), ((), ())), preferred_element_type=F32)


def dot_tn(a, b):
    return lax.dot_general(a, b, (((0,), (0,)), ((), ())), preferred_element_type=F32)


class Link:
    def __init__(self, send, recv):
        self.send, self.recv, self.started = send, recv, []

    def copy(self, k, src, dst, to):
        return pltpu.make_async_remote_copy(
            src_ref=src,
            dst_ref=dst,
            send_sem=self.send.at[k],
            recv_sem=self.recv.at[k],
            device_id=to,
            device_id_type=MESH,
        )

    def start(self, k, src, dst, to):
        cp = self.copy(k, src, dst, to)
        cp.start()
        self.started.append(cp)

    def arrived(self, k, dst, to):
        self.copy(k, dst, dst, to).wait_recv()

    def sent(self):
        for cp in self.started:
            cp.wait_send()
        self.started = []


class Gather:
    def __init__(self, link, slot, half, place, pair, ring, core):
        self.link, self.slot, self.half = link, slot, half
        self.p, self.r = place
        self.pair_dev, self.core_dev = pair, core
        self.next_dev, self.prev_dev = ring
        self.q = 1 - self.p
        self.nxt, self.prv, self.far = (self.r + 1) % 4, (self.r + 3) % 4, (self.r + 2) % 4
        self.shared = []

    def put(self, k, p, r, to):
        ref = self.slot(p, r)
        self.link.start(k, ref, ref, to)

    def put_half(self, k, p, r, h, to):
        ref = self.half(p, r, h)
        self.link.start(k, ref, ref, to)

    def got(self, k, p, r):
        self.link.arrived(k, self.slot(p, r), self.pair_dev)

    def got_half(self, k, p, r, h):
        self.link.arrived(k, self.half(p, r, h), self.pair_dev)

    def share(self, p, r):
        if self.core_dev is not None:
            self.put(9 + len(self.shared), p, r, self.core_dev)
            self.shared.append((p, r))

    def start_pair(self):
        self.put(0, self.p, self.r, self.pair_dev)

    def start_ring(self):
        self.put(1, self.p, self.r, self.next_dev)
        self.put(2, self.p, self.r, self.prev_dev)
        self.share(self.p, self.r)

    def on_pair(self):
        self.got(0, self.q, self.r)
        self.put(3, self.q, self.r, self.next_dev)
        self.put(4, self.q, self.r, self.prev_dev)
        self.share(self.q, self.r)

    def on_ring(self, p, base, k):
        self.got(base, p, self.prv)
        self.put_half(k, p, self.prv, 0, self.next_dev)
        self.share(p, self.prv)
        self.got(base + 1, p, self.nxt)
        self.put_half(k + 1, p, self.nxt, 1, self.prev_dev)
        self.share(p, self.nxt)

    def on_ring_own(self):
        self.on_ring(self.p, 1, 5)

    def on_ring_pair(self):
        self.on_ring(self.q, 3, 7)

    def on_far(self):
        for p, k in ((self.p, 5), (self.q, 7)):
            self.got_half(k, p, self.far, 0)
            self.got_half(k + 1, p, self.far, 1)
            self.share(p, self.far)

    def last_ring(self):
        self.got(1, self.p, self.prv)
        self.put_half(5, self.p, self.prv, 0, self.next_dev)
        self.put(3, self.p, self.prv, self.pair_dev)
        self.share(self.p, self.prv)
        self.got(2, self.p, self.nxt)
        self.put_half(6, self.p, self.nxt, 1, self.prev_dev)
        self.put(4, self.p, self.nxt, self.pair_dev)
        self.share(self.p, self.nxt)

    def last_far(self):
        self.got_half(5, self.p, self.far, 0)
        self.got_half(6, self.p, self.far, 1)
        self.put(7, self.p, self.far, self.pair_dev)
        self.share(self.p, self.far)

    def last_pair(self):
        for k, r in ((0, self.r), (3, self.prv), (4, self.nxt), (7, self.far)):
            self.got(k, self.q, r)
            self.share(self.q, r)

    def done(self, other_slot=None):
        for i, (p, r) in enumerate(self.shared):
            self.link.arrived(9 + i, other_slot(p, r), self.pair_dev)

    def sent(self):
        self.link.sent()


class Scatter:
    def __init__(self, link, parts, bufs, place, devs):
        self.link, self.parts = link, parts
        self.from_core, self.from_prev_half, self.from_next_half, self.from_prev, self.from_next, self.from_pair = bufs
        self.yl, self.z, self.c = place
        self.core_dev, self.pair_dev, self.next_dev, self.prev_dev = devs
        self.nxt, self.prv, self.far = (self.z + 1) % 4, (self.z + 3) % 4, (self.z + 2) % 4

    def give_core(self, ch):
        self.link.copy(
            ch, self.parts.at[ch, :, :, 1 - self.c], self.from_core.at[ch], self.core_dev
        ).start()

    def add_core(self):
        def step(ch, carry):
            self.link.copy(
                ch, self.parts.at[ch, :, :, 1 - self.c], self.from_core.at[ch], self.core_dev
            ).wait()
            own = self.parts[ch, :, :, self.c].astype(F32)
            self.parts[ch, :, :, self.c] = (own + self.from_core[ch].astype(F32)).astype(BF)
            return carry

        lax.fori_loop(0, CHUNKS, step, 0)

    def half(self, z, h):
        return self.parts.at[4 * h : 4 * h + 4, :, z, self.c]

    def start(self):
        link = self.link
        link.start(8, self.half(self.far, 0), self.from_prev_half, self.next_dev)
        link.start(9, self.half(self.far, 1), self.from_next_half, self.prev_dev)
        link.start(10, self.half(self.nxt, 1), self.from_prev.at[4:8], self.next_dev)
        link.start(11, self.half(self.prv, 0), self.from_next.at[0:4], self.prev_dev)

    def middle(self):
        link = self.link
        link.arrived(8, self.from_prev_half, self.pair_dev)
        for ch in range(4):
            mine = self.parts[ch, :, self.nxt, self.c].astype(F32)
            self.parts[ch, :, self.nxt, self.c] = (mine + self.from_prev_half[ch].astype(F32)).astype(BF)
        link.start(12, self.half(self.nxt, 0), self.from_prev.at[0:4], self.next_dev)
        link.arrived(9, self.from_next_half, self.pair_dev)
        for ch in range(4):
            mine = self.parts[4 + ch, :, self.prv, self.c].astype(F32)
            self.parts[4 + ch, :, self.prv, self.c] = (mine + self.from_next_half[ch].astype(F32)).astype(BF)
        link.start(13, self.half(self.prv, 1), self.from_next.at[4:8], self.prev_dev)

    def to_pair(self):
        link = self.link
        link.arrived(10, self.from_prev.at[4:8], self.pair_dev)
        link.arrived(11, self.from_next.at[0:4], self.pair_dev)
        for k, h in ((12, 0), (13, 1)):
            buf = self.from_prev if h == 0 else self.from_next
            link.arrived(k, buf.at[4 * h : 4 * h + 4], self.pair_dev)
            for ch in range(4 * h, 4 * h + 4):
                total = (
                    self.parts[ch, :, self.z, self.c].astype(F32)
                    + self.from_prev[ch].astype(F32)
                    + self.from_next[ch].astype(F32)
                )
                self.parts[ch, :, self.z, self.c] = total.astype(BF)
            link.start(
                14 + h,
                self.parts.at[4 * h : 4 * h + 4, 1 - self.yl, self.z, self.c],
                self.from_pair.at[4 * h : 4 * h + 4],
                self.pair_dev,
            )

    def arrived(self, h):
        self.link.arrived(14 + h, self.from_pair.at[4 * h : 4 * h + 4], self.pair_dev)

    def chunk(self, ch):
        return self.parts[ch, self.yl, self.z, self.c].astype(F32) + self.from_pair[ch].astype(F32)

    def sent(self):
        self.link.sent()


def layer(
    inputs_ref, gain_ref, doc_row_ref, doc_col_ref, freq_ref, wq_hbm, wkv_hbm, wo_hbm, gout_ref,
    out_ref, gin_ref, ggain_ref, gwq_ref, gwk_ref, gwv_ref, gwo_ref,
    xs, gs, nc, gc, wq, wkv, wo, att, qkv, acc, kvh, kvg, qh, probs,
    rs0, rs1, rs2, rs3, rs4, rs5, rt0, rt1, rt2, rt3, rt4, rt5,
    ga0, ga1, ga2,
    x_s, x_r, g_s, g_r, nc_s, nc_r, gc_s, gc_r, at_s, at_r, qk_s, qk_r, ro_s, ro_r, rg_s, rg_r,
    tn_s, tn_r, tg_s, tg_r, kv_s, kv_r, ga_s, ga_r, w_sem,
):
    dp, head = lax.axis_index("dp"), lax.axis_index("head")
    x, yh = dp // 2, dp % 2
    yl, z, c = head // 8, (head // 2) % 4, head % 2
    core_dev = device(x, yh, yl, z, 1 - c)
    pair_dev = device(x, yh, 1 - yl, z, c)
    z_dev = [device(x, yh, yl, (z + k) % 4, c) for k in range(4)]
    dp_devs = [((dp + k) % 8, head) for k in range(1, 8)]
    x_dev = [device((x + k) % 4, yh, yl, z, c) for k in range(4)]
    yh_dev = device(x, 1 - yh, yl, z, c)
    diag_dev = device(x, yh, 1 - yl, z, 1 - c)

    weights = [
        pltpu.make_async_copy(wq_hbm, wq, w_sem.at[0]),
        pltpu.make_async_copy(wkv_hbm, wkv, w_sem.at[1]),
        pltpu.make_async_copy(wo_hbm, wo, w_sem.at[2]),
    ]
    for cp in weights:
        cp.start()

    barrier = pltpu.get_barrier_semaphore()
    partners = [core_dev, pair_dev, diag_dev] + z_dev[1:] + dp_devs
    for to in partners:
        pl.semaphore_signal(barrier, inc=1, device_id=to, device_id_type=MESH)

    square = jnp.zeros((ROWS, 1), F32)
    for ch in range(CHUNKS):
        part = inputs_ref[:, ch * CHUNK : (ch + 1) * CHUNK].astype(F32)
        square += jnp.sum(part * part, axis=-1, keepdims=True)
    inverse_rms = lax.rsqrt(square * (1.0 / (CHUNKS * CHUNK)) + EPSILON)
    for ch in range(CHUNKS):
        cols = slice(ch * CHUNK, (ch + 1) * CHUNK)
        part = inputs_ref[:, cols].astype(F32)
        xs[ch, yl, z, c] = (part * inverse_rms * gain_ref[:, cols]).astype(BF)
        gs[ch, yl, z, c] = gout_ref[:, cols]
    nc[dp, yl, z, c] = xs[dp, yl, z, c]
    gc[dp, yl, z, c] = gs[dp, yl, z, c]

    pl.semaphore_wait(barrier, len(partners))

    def head_gather(buf, send, recv):
        return Gather(
            Link(send, recv),
            lambda p, r: buf.at[:, p, r, c],
            lambda p, r, h: buf.at[4 * h : 4 * h + 4, p, r, c],
            (yl, z), pair_dev, (z_dev[1], z_dev[3]), core_dev,
        )

    def other_core(buf):
        return lambda p, r: buf.at[:, p, r, 1 - c]

    def dp_gather(buf, send, recv):
        return Gather(
            Link(send, recv),
            lambda p, r: buf.at[r, p],
            lambda p, r, h: buf.at[r, p, 128 * h : 128 * h + 128],
            (yh, x), yh_dev, (x_dev[1], x_dev[3]), None,
        )

    gx, gg = head_gather(xs, x_s, x_r), head_gather(gs, g_s, g_r)
    gnc, ggc = head_gather(nc, nc_s, nc_r), head_gather(gc, gc_s, gc_r)
    gat, gqk = dp_gather(att, at_s, at_r), dp_gather(qkv, qk_s, qk_r)
    devs = (core_dev, pair_dev, z_dev[1], z_dev[3])
    ro = Scatter(Link(ro_s, ro_r), xs, (rs0, rs1, rs2, rs3, rs4, rs5), (yl, z, c), devs)
    rg = Scatter(Link(rg_s, rg_r), gs, (rt0, rt1, rt2, rt3, rt4, rt5), (yl, z, c), devs)

    gx.start_ring()
    gx.start_pair()
    gg.start_pair()
    tiny_n, tiny_g = Link(tn_s, tn_r), Link(tg_s, tg_r)
    for link, src, dst in ((tiny_n, xs, nc), (tiny_g, gs, gc)):
        for k in range(1, 8):
            to = (dp + k) % 8
            link.start(k - 1, src.at[to, yl, z, c], dst.at[dp, yl, z, c], (to, head))

    row_index = lax.broadcasted_iota(jnp.int32, (SEQ, SEQ), 0)
    col_index = lax.broadcasted_iota(jnp.int32, (SEQ, SEQ), 1)
    same = doc_col_ref[...] == doc_row_ref[...]
    allowed = same & (col_index <= row_index)
    position = jnp.sum(jnp.where(allowed, 1.0, 0.0), axis=-1, keepdims=True) - 1.0
    angles = position * freq_ref[...]
    cosine, sine = jnp.cos(angles), jnp.sin(angles)
    lane = lax.broadcasted_iota(jnp.int32, (SEQ, HD), 1)
    low_half = lane < HD // 2
    sine_turn = jnp.where(low_half, -sine, sine)

    def rope(u):
        return u * cosine + pltpu.roll(u, HD // 2, 1) * sine_turn

    def rope_back(g):
        turned = pltpu.roll(g * sine, HD // 2, 1)
        return g * cosine + jnp.where(low_half, turned, -turned)

    gx.on_pair()
    gx.on_ring_own()
    gx.on_ring_pair()
    gg.start_ring()
    gg.on_pair()
    gx.on_far()
    gx.done(other_core(xs))

    weights[0].wait()
    weights[1].wait()

    def project(ch, carry):
        block = xs[ch].reshape(SEQ, CHUNK)
        rows = pl.ds(pl.multiple_of(ch * CHUNK, CHUNK), CHUNK)
        acc[...] += dot(block, wq[rows, :])
        kvh_acc[...] += dot(block, wkv[rows, :])
        return carry

    kvh_acc = probs.at[0, :, 0:HD]
    acc[...] = jnp.zeros_like(acc)
    kvh_acc[...] = jnp.zeros((SEQ, HD), F32)
    lax.fori_loop(0, CHUNKS, project, 0)
    kvh[c] = kvh_acc[...].astype(BF)
    kv_link = Link(kv_s, kv_r)
    kv_link.start(0, kvh.at[c], kvh.at[c], core_dev)
    for h in range(HEADS):
        pre = acc[:, h * HD : (h + 1) * HD].astype(BF).astype(F32)
        qh[h] = rope(pre).astype(BF)
    gg.on_ring_own()
    gg.on_ring_pair()
    kv_link.arrived(0, kvh.at[1 - c], core_dev)
    first, second = kvh[0].astype(F32), kvh[1].astype(F32)
    key_pre = jnp.where(low_half, first, pltpu.roll(second, HD // 2, 1))
    values = jnp.where(low_half, pltpu.roll(first, HD // 2, 1), second).astype(BF)
    key_rows = rope(key_pre).astype(BF)
    score_scale = HD ** (-0.5)

    for h in range(HEADS):
        scores = dot_nt(qh[h], key_rows) * score_scale
        scores = jnp.where(allowed, scores, -1e30)
        top = jnp.max(scores, axis=-1, keepdims=True)
        e = jnp.exp(scores - top)
        p = e / jnp.sum(e, axis=-1, keepdims=True)
        probs[h] = p
        att[x, yh, :, h * HD : (h + 1) * HD] = dot(p.astype(BF), values).astype(BF)
    gat.start_ring()
    gat.start_pair()

    gx.sent()
    tiny_n.sent()
    weights[2].wait()
    wide = (2, 4, 2, ROWS, CHUNK)

    def project_out(ch, carry):
        cols = pl.ds(pl.multiple_of(ch * CHUNK, CHUNK), CHUNK)
        xs[ch] = dot(att[x, yh], wo[:, cols]).astype(BF).reshape(wide)
        ro.give_core(ch)
        return carry

    lax.fori_loop(0, CHUNKS, project_out, 0)
    gg.on_far()
    gg.done(other_core(gs))
    ro.add_core()
    ro.start()

    acc[...] = jnp.zeros_like(acc)

    def back_out(ch, carry):
        cols = pl.ds(pl.multiple_of(ch * CHUNK, CHUNK), CHUNK)
        acc[...] += dot_nt(gs[ch].reshape(SEQ, CHUNK), wo[:, cols])
        return carry

    lax.fori_loop(0, CHUNKS, back_out, 0)
    gat.on_pair()
    ro.middle()
    key_sum = jnp.zeros((SEQ, HD), F32)
    value_sum = jnp.zeros((SEQ, HD), F32)
    for h in range(HEADS):
        grad_att = acc[:, h * HD : (h + 1) * HD].astype(BF)
        p = probs[h]
        grad_probs = dot_nt(grad_att, values)
        delta = jnp.sum(p * grad_probs, axis=-1, keepdims=True)
        grad_scores = (p * (grad_probs - delta)).astype(BF)
        grad_query = dot(grad_scores, key_rows) * score_scale
        qkv[x, yh, :, h * HD : (h + 1) * HD] = rope_back(grad_query).astype(BF)
        key_sum += dot_tn(grad_scores, qh[h])
        value_sum += dot_tn(p.astype(BF), grad_att)
    kvg[c, 0] = rope_back(key_sum * score_scale).astype(BF)
    kvg[c, 1] = value_sum.astype(BF)
    kv_link.start(1, kvg.at[c], kvg.at[c], core_dev)
    gat.on_ring_own()
    gat.on_ring_pair()
    kv_link.arrived(1, kvg.at[1 - c], core_dev)
    key_pair = (kvg[0, 0].astype(F32) + kvg[1, 0].astype(F32)).astype(BF).astype(F32)
    value_pair = (kvg[0, 1].astype(F32) + kvg[1, 1].astype(F32)).astype(BF).astype(F32)
    even = jnp.where(low_half, key_pair, pltpu.roll(value_pair, HD // 2, 1))
    odd = jnp.where(low_half, pltpu.roll(key_pair, HD // 2, 1), value_pair)
    qkv[x, yh, :, HEADS * HD :] = jnp.where(c == 0, even, odd).astype(BF)
    gqk.start_ring()
    gqk.start_pair()

    gg.sent()
    tiny_g.sent()

    def back_in(ch, carry):
        rows = pl.ds(pl.multiple_of(ch * CHUNK, CHUNK), CHUNK)
        part = dot_nt(qkv[x, yh, :, : HEADS * HD], wq[rows, :])
        part += dot_nt(qkv[x, yh, :, HEADS * HD :], wkv[rows, :])
        gs[ch] = part.astype(BF).reshape(wide)
        rg.give_core(ch)
        return carry

    lax.fori_loop(0, CHUNKS, back_in, 0)
    ro.to_pair()
    rg.add_core()
    rg.start()

    for link, dst in ((tiny_n, nc), (tiny_g, gc)):
        for k in range(1, 8):
            link.arrived(k - 1, dst.at[(dp + 8 - k) % 8, yl, z, c], core_dev)
    gnc.start_ring()
    gnc.start_pair()
    ggc.start_ring()
    ggc.start_pair()
    gat.on_far()
    gqk.on_pair()
    rg.middle()
    gqk.on_ring_own()
    gqk.on_ring_pair()
    for h in range(2):
        ro.arrived(h)
        for ch in range(4 * h, 4 * h + 4):
            cols = slice(ch * CHUNK, (ch + 1) * CHUNK)
            out_ref[:, cols] = (inputs_ref[:, cols].astype(F32) + ro.chunk(ch)).astype(BF)
    gqk.on_far()
    rg.to_pair()
    gnc.last_ring()
    ggc.last_ring()

    mean = jnp.zeros((ROWS, 1), F32)
    gain_slot = yl * 2 + c
    for h in range(2):
        rg.arrived(h)
        for ch in range(4 * h, 4 * h + 4):
            cols = slice(ch * CHUNK, (ch + 1) * CHUNK)
            grad = rg.chunk(ch)
            part = inputs_ref[:, cols].astype(F32)
            ga0[gain_slot, ch : ch + 1] = jnp.sum(grad * part * inverse_rms, axis=0, keepdims=True)
            mean += jnp.sum(grad * gain_ref[:, cols] * part, axis=-1, keepdims=True)
    ga_link = Link(ga_s, ga_r)
    near = [(core_dev, yl * 2 + 1 - c), (pair_dev, (1 - yl) * 2 + c), (diag_dev, (1 - yl) * 2 + 1 - c)]
    for k, (to, _) in enumerate(near):
        ga_link.start(k, ga0.at[gain_slot], ga0.at[gain_slot], to)
    mean = mean * (1.0 / (CHUNKS * CHUNK)) * inverse_rms * inverse_rms * inverse_rms
    for ch in range(CHUNKS):
        cols = slice(ch * CHUNK, (ch + 1) * CHUNK)
        part = inputs_ref[:, cols].astype(F32)
        scaled = rg.chunk(ch) * gain_ref[:, cols]
        gin_ref[:, cols] = (gout_ref[:, cols].astype(F32) + inverse_rms * scaled - part * mean).astype(BF)
    gnc.last_far()
    ggc.last_far()
    for k, (_, slot) in enumerate(near):
        ga_link.arrived(k, ga0.at[slot], core_dev)
    ga1[z] = (ga0[0] + ga0[1]) + (ga0[2] + ga0[3])
    for k in range(1, 4):
        ga_link.start(2 + k, ga1.at[z], ga1.at[z], z_dev[k])

    gnc.last_pair()
    ggc.last_pair()
    for k in range(1, 4):
        ga_link.arrived(2 + k, ga1.at[(z + 4 - k) % 4], core_dev)
    ga2[dp] = (ga1[0] + ga1[1]) + (ga1[2] + ga1[3])
    for k in range(1, 8):
        ga_link.start(5 + k, ga2.at[dp], ga2.at[dp], ((dp + k) % 8, head))

    gnc.done(other_core(nc))
    total = None
    for s in range(8):
        term = dot_tn(nc[s].reshape(SEQ, CHUNK), qkv[s // 2, s % 2])
        total = term if total is None else total + term
    gwq_ref[...] = total[:, : HEADS * HD].astype(BF)
    gwk_ref[...] = total[:, HEADS * HD : HEADS * HD + HD // 2].astype(BF)
    gwv_ref[...] = total[:, HEADS * HD + HD // 2 :].astype(BF)
    ggc.done(other_core(gc))
    total = None
    for s in range(8):
        term = dot_tn(att[s // 2, s % 2], gc[s].reshape(SEQ, CHUNK))
        total = term if total is None else total + term
    gwo_ref[...] = total.astype(BF)

    for k in range(1, 8):
        ga_link.arrived(5 + k, ga2.at[(dp + 8 - k) % 8], core_dev)
    ggain_ref[...] = ((ga2[0] + ga2[1]) + (ga2[2] + ga2[3])) + ((ga2[4] + ga2[5]) + (ga2[6] + ga2[7]))

    for link in (gat, gqk, gnc, ggc, ro, rg, kv_link, ga_link):
        link.sent()


def per_device(inputs, gain, doc_ids, w_query, w_key, w_value, w_out, grad_out):
    w_kv = jnp.concatenate([w_key, w_value], axis=1)
    exponent = jnp.arange(HD // 2, dtype=F32) * (2.0 / HD)
    frequency = THETA ** (-exponent)
    frequency = jnp.concatenate([frequency, frequency])[None, :]
    vmem = pl.BlockSpec(memory_space=pltpu.VMEM)
    hbm = pl.BlockSpec(memory_space=pl.ANY)
    rows = (CHUNKS, 2, 4, 2, ROWS, CHUNK)
    half = (4, 2, ROWS, CHUNK)
    scatter = [
        pltpu.VMEM((CHUNKS, 2, 4, ROWS, CHUNK), BF),
        pltpu.VMEM(half, BF),
        pltpu.VMEM(half, BF),
        pltpu.VMEM((CHUNKS, 2, ROWS, CHUNK), BF),
        pltpu.VMEM((CHUNKS, 2, ROWS, CHUNK), BF),
        pltpu.VMEM((CHUNKS, ROWS, CHUNK), BF),
    ]
    dma = lambda n: [pltpu.SemaphoreType.DMA((n,))] * 2
    outs = pl.pallas_call(
        layer,
        out_shape=(
            jax.ShapeDtypeStruct((ROWS, CHUNKS * CHUNK), BF),
            jax.ShapeDtypeStruct((ROWS, CHUNKS * CHUNK), BF),
            jax.ShapeDtypeStruct((CHUNKS, CHUNK), F32),
            jax.ShapeDtypeStruct((CHUNK, HEADS * HD), BF),
            jax.ShapeDtypeStruct((CHUNK, HD // 2), BF),
            jax.ShapeDtypeStruct((CHUNK, HD // 2), BF),
            jax.ShapeDtypeStruct((HEADS * HD, CHUNK), BF),
        ),
        in_specs=[vmem] * 5 + [hbm] * 3 + [vmem],
        out_specs=[vmem] * 7,
        scratch_shapes=[
            pltpu.VMEM(rows, BF),
            pltpu.VMEM(rows, BF),
            pltpu.VMEM(rows, BF),
            pltpu.VMEM(rows, BF),
            pltpu.VMEM((CHUNKS * CHUNK, HEADS * HD), BF),
            pltpu.VMEM((CHUNKS * CHUNK, HD), BF),
            pltpu.VMEM((HEADS * HD, CHUNKS * CHUNK), BF),
            pltpu.VMEM((4, 2, SEQ, HEADS * HD), BF),
            pltpu.VMEM((4, 2, SEQ, HEADS * HD + HD), BF),
            pltpu.VMEM((SEQ, HEADS * HD), F32),
            pltpu.VMEM((2, SEQ, HD), BF),
            pltpu.VMEM((2, 2, SEQ, HD), BF),
            pltpu.VMEM((HEADS, SEQ, HD), BF),
            pltpu.VMEM((HEADS, SEQ, SEQ), F32),
        ]
        + scatter
        + scatter
        + [
            pltpu.VMEM((4, CHUNKS, CHUNK), F32),
            pltpu.VMEM((4, CHUNKS, CHUNK), F32),
            pltpu.VMEM((8, CHUNKS, CHUNK), F32),
        ]
        + dma(17) * 4
        + dma(9) * 2
        + dma(16) * 2
        + dma(7) * 2
        + dma(2)
        + dma(13)
        + [pltpu.SemaphoreType.DMA((3,))],
        compiler_params=pltpu.CompilerParams(
            collective_id=0, has_side_effects=True, vmem_limit_bytes=60 * 2**20
        ),
    )(
        inputs,
        gain[None, :],
        doc_ids,
        doc_ids.reshape(SEQ, 1),
        frequency,
        w_query,
        w_kv,
        w_out,
        grad_out,
    )
    out, gin, ggain, gwq, gwk, gwv, gwo = outs
    return (out, gin, ggain.reshape(-1), gwq, gwk, gwv, gwo)


def solution(mesh):
    return jax.shard_map(
        per_device,
        mesh=mesh,
        in_specs=(
            P(("dp", "head"), None),
            P(),
            P("dp", None),
            P(None, "head"),
            P(None, "head"),
            P(None, "head"),
            P("head", None),
            P(("dp", "head"), None),
        ),
        out_specs=(
            P(("dp", "head"), None),
            P(("dp", "head"), None),
            P(),
            P("dp", "head"),
            P("dp", "head"),
            P("dp", "head"),
            P("head", "dp"),
        ),
        check_vma=False,
    )
```

time: 573 us -> 182 us (0.32)
  waiting for transfers between devices: 396 us -> 0 us
  Pallas kernels: 0 us -> 159 us
  blocking collectives: 69.6 us -> 0 us
  matrix products: 65.6 us -> 0 us
  other arithmetic: 18.7 us -> 4.69 us
  between operations: 14.4 us -> 0.68 us
  local copies, waits for them, and re-layouts: 5.32 us -> 16.2 us
    reduce_scatter x5 -> x0, waiting for transfers between devices: 333 us -> none  [the longest x1 118 us: per_device(): lax.psum_scatter(partial_out.astype(jnp.bfloat16), 'dp', scatter_dimensio...]
    pallas_call x0 -> x1, Pallas kernels: none -> 159 us  [per_device(): pl.pallas_call(layer, out_shape=(jax.ShapeDtypeStruct((ROWS, CHUNKS * CHU...]
    psum x1 -> x0, blocking collectives: 69.6 us -> none  [per_device(): grad_gain = lax.psum(gain_part, ('dp', 'head'))]
    dot_general x16 -> x0, matrix products: 64.2 us -> none  [the longest x3 18.4 us: over_rows(): lax.dot_general(left, right, (((0,), (0,)), ((), ())), preferred_element_...]
    all_gather x2 -> x0, waiting for transfers between devices: 58.6 us -> none  [the longest x1 31.9 us: per_device(): normed_all = lax.all_gather(normed, 'head', axis=0, tiled=True)]
    unnamed x30 -> x15, local copies, waits for them, and re-layouts: 2.92 us -> 15.4 us
  transfers between devices with their start and end apart: 9 -> 0, of which waited for: 8 -> 0; matrix products, arithmetic and copies ran while one was open for 11% -> 0% of each run, Pallas kernels for 0% -> 0%
where the time goes in v1:
time: 182 us; the launch traced here: 181 us
  Pallas kernels  159 us (87%)
  local copies, waits for them, and re-layouts  16.2 us (9%)
  other arithmetic  4.69 us (3%)
    pallas_call x1, Pallas kernels, per_device(): pl.pallas_call(layer, out_shape=(jax.ShapeDtypeStruct((ROWS, CHUNKS * CHU...  159 us
    unnamed x15, local copies, waits for them, and re-layouts  15.4 us
    concatenate x1, other arithmetic, per_device(): w_kv = jnp.concatenate([w_key, w_value], axis=1)  4.08 us

profile of v1, /device:TPU:1, one launch (start us, length us, event | category | flops | bytes accessed | tf_op | source)
XLA Modules:
  0.0 180.7 jit_solution(14015677515576627591)
XLA Ops:
  0.6 0.0 copy-start
  0.6 2.1 %copy.19 = bf16[8192,64]{1,0:T(8,128)(2,1)S(1)} copy(bf16[8192,64]{0,1:T(8,128)(2,1)} %param.12) | data formatting | bytes 2097152 | tf_op args[4]
  2.8 0.0 copy-done
  2.8 1.8 copy.20
  4.6 0.0 copy-start.2
  4.6 4.1 %pad_maximum_fusion.wkv_hbm = bf16[8192,128]{1,0:T(8,128)(2,1)} fusion(bf16[8192,64]{1,0:T(8,128)(2,1)} %copy.20, bf16[8192,64]{1,0:T(8,128)(2,1)S(1)} %copy.19), kind=kLoop, calls=%fused_computation | loop fusion | flops 4194304 | bytes 4194304 | tf_op jit(solution)/shard_map/concatenate | solution.py:538
  8.6 0.0 copy-done.2
  8.6 0.8 copy.21.doc_col_ref
  9.5 0.6 maximum_bitcast_fusion.freq_ref
  10.0 159.2 %shard_map.135 = (bf16[16,8192]{1,0:T(8,128)(2,1)}, bf16[16,8192]{1,0:T(8,128)(2,1)}, f32[8,1024]{1,0:T(8,128)}, bf16[1024,512]{1,0:T(8,128)(2,1)}, bf16[1024,64...) custom-call(bf16[16,8192]{1,0:T(8,128)(2,1)} %inputs_ref.1, f32[1,8192]{1,0:T(1,128)} %bitcast.8, ...), custom_call_target="tpu_custom_call" | custom-call | tf_op jit(solution)/shard_map/pallas_call | solution.py:555
  169.2 0.0 copy-start.1
  169.2 1.8 %copy.22 = bf16[1024,64]{0,1:T(8,128)(2,1)} copy(bf16[1024,64]{1,0:T(8,128)(2,1)} %get-tuple-element.32) | data formatting | bytes 262144
  171.0 1.7 copy.23
  172.8 1.4 copy.26
  174.1 1.7 copy.31
  175.8 1.7 copy.32
  177.5 2.3 %copy.33 = bf16[1024,512]{1,0:T(8,128)(2,1)} copy(bf16[1024,512]{1,0:T(8,128)(2,1)} %get-tuple-element.45) | data formatting | bytes 2097152
  179.7 0.0 copy-done.1
  179.7 1.0 copy.34
  (1 shorter events, 0.0 us)
Async XLA Ops:
  0.6 2.1 %copy-start = (bf16[8192,64]{0,1:T(8,128)(2,1)S(1)}, bf16[8192,64]{0,1:T(8,128)(2,1)}, u32[]{:S(2)}) copy-start(bf16[8192,64]{0,1:T(8,128)(2,1)} %param.13) | copy-start | bytes 3145732
  4.6 4.1 %copy-start.2 = (s32[1,256]{1,0:T(1,128)S(1)}, s32[1,256]{1,0:T(1,128)}, u32[]{:S(2)}) copy-start(s32[1,256]{1,0:T(1,128)} %doc_row_ref.1) | copy-start | bytes 3076
  169.2 10.5 %copy-start.1 = (bf16[512,1024]{1,0:T(8,128)(2,1)S(1)}, bf16[512,1024]{1,0:T(8,128)(2,1)}, u32[]{:S(2)}) copy-start(bf16[512,1024]{1,0:T(8,128)(2,1)} %get-tuple-element.48) | copy-start | bytes 3145732

commit v2 on v1

--- a/solution.py
+++ b/solution.py
@@ -1,4 +1,4 @@
-import functools
+import math
 
 import jax
 import jax.numpy as jnp
@@ -8,7 +8,7 @@
 from jax.sharding import PartitionSpec as P
 
 EPSILON = 1e-05
-THETA = 500000.0
+LOG_THETA = math.log(500000.0)
 MESH = pl.DeviceIdType.MESH
 BF = jnp.bfloat16
 F32 = jnp.float32
@@ -236,13 +236,13 @@
 
 
 def layer(
-    inputs_ref, gain_ref, doc_row_ref, doc_col_ref, freq_ref, wq_hbm, wkv_hbm, wo_hbm, gout_ref,
+    inputs_ref, gain_ref, doc_ref, wq_hbm, wk_hbm, wv_hbm, wo_hbm, gout_ref,
     out_ref, gin_ref, ggain_ref, gwq_ref, gwk_ref, gwv_ref, gwo_ref,
-    xs, gs, nc, gc, wq, wkv, wo, att, qkv, acc, kvh, kvg, qh, probs,
-    rs0, rs1, rs2, rs3, rs4, rs5, rt0, rt1, rt2, rt3, rt4, rt5,
+    xs, gs, nc, gc, pg, wq, wkv, wo, att, qkv, acc, kvh, kvg, qh, probs,
+    rs0, rs1, rs2, rs3, rs4, rs5, rt1, rt2, rt3, rt4, rt5,
     ga0, ga1, ga2,
     x_s, x_r, g_s, g_r, nc_s, nc_r, gc_s, gc_r, at_s, at_r, qk_s, qk_r, ro_s, ro_r, rg_s, rg_r,
-    tn_s, tn_r, tg_s, tg_r, kv_s, kv_r, ga_s, ga_r, w_sem,
+    tn_s, tn_r, kv_s, kv_r, ga_s, ga_r, w_sem,
 ):
     dp, head = lax.axis_index("dp"), lax.axis_index("head")
     x, yh = dp // 2, dp % 2
@@ -257,8 +257,9 @@
 
     weights = [
         pltpu.make_async_copy(wq_hbm, wq, w_sem.at[0]),
-        pltpu.make_async_copy(wkv_hbm, wkv, w_sem.at[1]),
-        pltpu.make_async_copy(wo_hbm, wo, w_sem.at[2]),
+        pltpu.make_async_copy(wk_hbm, wkv.at[0 : HD // 2], w_sem.at[1]),
+        pltpu.make_async_copy(wv_hbm, wkv.at[HD // 2 : HD], w_sem.at[2]),
+        pltpu.make_async_copy(wo_hbm, wo, w_sem.at[3]),
     ]
     for cp in weights:
         cp.start()
@@ -279,7 +280,6 @@
         xs[ch, yl, z, c] = (part * inverse_rms * gain_ref[:, cols]).astype(BF)
         gs[ch, yl, z, c] = gout_ref[:, cols]
     nc[dp, yl, z, c] = xs[dp, yl, z, c]
-    gc[dp, yl, z, c] = gs[dp, yl, z, c]
 
     pl.semaphore_wait(barrier, len(partners))
 
@@ -303,30 +303,32 @@
         )
 
     gx, gg = head_gather(xs, x_s, x_r), head_gather(gs, g_s, g_r)
-    gnc, ggc = head_gather(nc, nc_s, nc_r), head_gather(gc, gc_s, gc_r)
+    gnc = head_gather(nc, nc_s, nc_r)
+    cols = Link(gc_s, gc_r)
     gat, gqk = dp_gather(att, at_s, at_r), dp_gather(qkv, qk_s, qk_r)
     devs = (core_dev, pair_dev, z_dev[1], z_dev[3])
     ro = Scatter(Link(ro_s, ro_r), xs, (rs0, rs1, rs2, rs3, rs4, rs5), (yl, z, c), devs)
-    rg = Scatter(Link(rg_s, rg_r), gs, (rt0, rt1, rt2, rt3, rt4, rt5), (yl, z, c), devs)
+    rg = Scatter(Link(rg_s, rg_r), pg, (rs0, rt1, rt2, rt3, rt4, rt5), (yl, z, c), devs)
 
     gx.start_ring()
     gx.start_pair()
     gg.start_pair()
-    tiny_n, tiny_g = Link(tn_s, tn_r), Link(tg_s, tg_r)
-    for link, src, dst in ((tiny_n, xs, nc), (tiny_g, gs, gc)):
-        for k in range(1, 8):
-            to = (dp + k) % 8
-            link.start(k - 1, src.at[to, yl, z, c], dst.at[dp, yl, z, c], (to, head))
+    tiny = Link(tn_s, tn_r)
+    for k in range(1, 8):
+        to = (dp + k) % 8
+        tiny.start(k - 1, xs.at[to, yl, z, c], nc.at[dp, yl, z, c], (to, head))
 
     row_index = lax.broadcasted_iota(jnp.int32, (SEQ, SEQ), 0)
     col_index = lax.broadcasted_iota(jnp.int32, (SEQ, SEQ), 1)
-    same = doc_col_ref[...] == doc_row_ref[...]
+    doc_rows = jnp.broadcast_to(doc_ref[...].astype(F32), (SEQ, SEQ))
+    same = doc_rows == doc_rows.T
     allowed = same & (col_index <= row_index)
     position = jnp.sum(jnp.where(allowed, 1.0, 0.0), axis=-1, keepdims=True) - 1.0
-    angles = position * freq_ref[...]
-    cosine, sine = jnp.cos(angles), jnp.sin(angles)
     lane = lax.broadcasted_iota(jnp.int32, (SEQ, HD), 1)
     low_half = lane < HD // 2
+    exponent = jnp.where(low_half, lane, lane - HD // 2).astype(F32) * (2.0 / HD)
+    angles = position * jnp.exp(exponent * -LOG_THETA)
+    cosine, sine = jnp.cos(angles), jnp.sin(angles)
     sine_turn = jnp.where(low_half, -sine, sine)
 
     def rope(u):
@@ -344,14 +346,14 @@
     gx.on_far()
     gx.done(other_core(xs))
 
-    weights[0].wait()
-    weights[1].wait()
+    for cp in weights[:3]:
+        cp.wait()
 
     def project(ch, carry):
         block = xs[ch].reshape(SEQ, CHUNK)
         rows = pl.ds(pl.multiple_of(ch * CHUNK, CHUNK), CHUNK)
         acc[...] += dot(block, wq[rows, :])
-        kvh_acc[...] += dot(block, wkv[rows, :])
+        kvh_acc[...] += dot_nt(block, wkv[:, rows])
         return carry
 
     kvh_acc = probs.at[0, :, 0:HD]
@@ -361,11 +363,10 @@
     kvh[c] = kvh_acc[...].astype(BF)
     kv_link = Link(kv_s, kv_r)
     kv_link.start(0, kvh.at[c], kvh.at[c], core_dev)
+    gg.on_ring_own()
     for h in range(HEADS):
         pre = acc[:, h * HD : (h + 1) * HD].astype(BF).astype(F32)
         qh[h] = rope(pre).astype(BF)
-    gg.on_ring_own()
-    gg.on_ring_pair()
     kv_link.arrived(0, kvh.at[1 - c], core_dev)
     first, second = kvh[0].astype(F32), kvh[1].astype(F32)
     key_pre = jnp.where(low_half, first, pltpu.roll(second, HD // 2, 1))
@@ -383,34 +384,43 @@
         att[x, yh, :, h * HD : (h + 1) * HD] = dot(p.astype(BF), values).astype(BF)
     gat.start_ring()
     gat.start_pair()
+    gg.on_ring_pair()
 
     gx.sent()
-    tiny_n.sent()
-    weights[2].wait()
+    tiny.sent()
+    weights[3].wait()
     wide = (2, 4, 2, ROWS, CHUNK)
 
     def project_out(ch, carry):
-        cols = pl.ds(pl.multiple_of(ch * CHUNK, CHUNK), CHUNK)
-        xs[ch] = dot(att[x, yh], wo[:, cols]).astype(BF).reshape(wide)
+        cols_ch = pl.ds(pl.multiple_of(ch * CHUNK, CHUNK), CHUNK)
+        xs[ch] = dot(att[x, yh], wo[:, cols_ch]).astype(BF).reshape(wide)
         ro.give_core(ch)
         return carry
 
     lax.fori_loop(0, CHUNKS, project_out, 0)
+    ro.add_core()
     gg.on_far()
+    ro.start()
+    gat.on_pair()
     gg.done(other_core(gs))
-    ro.add_core()
-    ro.start()
+
+    for k in range(1, 8):
+        to = (dp + k) % 8
+        cols.start(k - 1, gs.at[to, :, :, c], gc.at[dp, :, :, c], (to, head))
+    gc[dp] = gs[dp]
+    for k in range(1, 8):
+        tiny.arrived(k - 1, nc.at[(dp + 8 - k) % 8, yl, z, c], core_dev)
+    gnc.start_pair()
 
     acc[...] = jnp.zeros_like(acc)
 
     def back_out(ch, carry):
-        cols = pl.ds(pl.multiple_of(ch * CHUNK, CHUNK), CHUNK)
-        acc[...] += dot_nt(gs[ch].reshape(SEQ, CHUNK), wo[:, cols])
+        cols_ch = pl.ds(pl.multiple_of(ch * CHUNK, CHUNK), CHUNK)
+        acc[...] += dot_nt(gs[ch].reshape(SEQ, CHUNK), wo[:, cols_ch])
         return carry
 
     lax.fori_loop(0, CHUNKS, back_out, 0)
-    gat.on_pair()
-    ro.middle()
+    gat.on_ring_own()
     key_sum = jnp.zeros((SEQ, HD), F32)
     value_sum = jnp.zeros((SEQ, HD), F32)
     for h in range(HEADS):
@@ -426,8 +436,7 @@
     kvg[c, 0] = rope_back(key_sum * score_scale).astype(BF)
     kvg[c, 1] = value_sum.astype(BF)
     kv_link.start(1, kvg.at[c], kvg.at[c], core_dev)
-    gat.on_ring_own()
-    gat.on_ring_pair()
+    ro.middle()
     kv_link.arrived(1, kvg.at[1 - c], core_dev)
     key_pair = (kvg[0, 0].astype(F32) + kvg[1, 0].astype(F32)).astype(BF).astype(F32)
     value_pair = (kvg[0, 1].astype(F32) + kvg[1, 1].astype(F32)).astype(BF).astype(F32)
@@ -436,67 +445,59 @@
     qkv[x, yh, :, HEADS * HD :] = jnp.where(c == 0, even, odd).astype(BF)
     gqk.start_ring()
     gqk.start_pair()
-
-    gg.sent()
-    tiny_g.sent()
+    gat.on_ring_pair()
 
     def back_in(ch, carry):
         rows = pl.ds(pl.multiple_of(ch * CHUNK, CHUNK), CHUNK)
         part = dot_nt(qkv[x, yh, :, : HEADS * HD], wq[rows, :])
-        part += dot_nt(qkv[x, yh, :, HEADS * HD :], wkv[rows, :])
-        gs[ch] = part.astype(BF).reshape(wide)
+        part += dot(qkv[x, yh, :, HEADS * HD :], wkv[:, rows])
+        pg[ch] = part.astype(BF).reshape(wide)
         rg.give_core(ch)
         return carry
 
     lax.fori_loop(0, CHUNKS, back_in, 0)
-    ro.to_pair()
     rg.add_core()
     rg.start()
-
-    for link, dst in ((tiny_n, nc), (tiny_g, gc)):
-        for k in range(1, 8):
-            link.arrived(k - 1, dst.at[(dp + 8 - k) % 8, yl, z, c], core_dev)
     gnc.start_ring()
-    gnc.start_pair()
-    ggc.start_ring()
-    ggc.start_pair()
+    gqk.on_pair()
+    ro.to_pair()
     gat.on_far()
-    gqk.on_pair()
+    gqk.on_ring_own()
     rg.middle()
-    gqk.on_ring_own()
-    gqk.on_ring_pair()
     for h in range(2):
         ro.arrived(h)
         for ch in range(4 * h, 4 * h + 4):
-            cols = slice(ch * CHUNK, (ch + 1) * CHUNK)
-            out_ref[:, cols] = (inputs_ref[:, cols].astype(F32) + ro.chunk(ch)).astype(BF)
-    gqk.on_far()
+            span = slice(ch * CHUNK, (ch + 1) * CHUNK)
+            out_ref[:, span] = (inputs_ref[:, span].astype(F32) + ro.chunk(ch)).astype(BF)
+    gqk.on_ring_pair()
+    gnc.last_ring()
+    for k in range(1, 8):
+        block = gc.at[(dp + 8 - k) % 8, :, :, c]
+        cols.arrived(k - 1, block, core_dev)
+        cols.start(6 + k, block, block, core_dev)
     rg.to_pair()
-    gnc.last_ring()
-    ggc.last_ring()
+    gnc.last_far()
 
     mean = jnp.zeros((ROWS, 1), F32)
     gain_slot = yl * 2 + c
     for h in range(2):
         rg.arrived(h)
         for ch in range(4 * h, 4 * h + 4):
-            cols = slice(ch * CHUNK, (ch + 1) * CHUNK)
+            span = slice(ch * CHUNK, (ch + 1) * CHUNK)
             grad = rg.chunk(ch)
-            part = inputs_ref[:, cols].astype(F32)
+            part = inputs_ref[:, span].astype(F32)
             ga0[gain_slot, ch : ch + 1] = jnp.sum(grad * part * inverse_rms, axis=0, keepdims=True)
-            mean += jnp.sum(grad * gain_ref[:, cols] * part, axis=-1, keepdims=True)
+            mean += jnp.sum(grad * gain_ref[:, span] * part, axis=-1, keepdims=True)
     ga_link = Link(ga_s, ga_r)
     near = [(core_dev, yl * 2 + 1 - c), (pair_dev, (1 - yl) * 2 + c), (diag_dev, (1 - yl) * 2 + 1 - c)]
     for k, (to, _) in enumerate(near):
         ga_link.start(k, ga0.at[gain_slot], ga0.at[gain_slot], to)
     mean = mean * (1.0 / (CHUNKS * CHUNK)) * inverse_rms * inverse_rms * inverse_rms
     for ch in range(CHUNKS):
-        cols = slice(ch * CHUNK, (ch + 1) * CHUNK)
-        part = inputs_ref[:, cols].astype(F32)
-        scaled = rg.chunk(ch) * gain_ref[:, cols]
-        gin_ref[:, cols] = (gout_ref[:, cols].astype(F32) + inverse_rms * scaled - part * mean).astype(BF)
-    gnc.last_far()
-    ggc.last_far()
+        span = slice(ch * CHUNK, (ch + 1) * CHUNK)
+        part = inputs_ref[:, span].astype(F32)
+        scaled = rg.chunk(ch) * gain_ref[:, span]
+        gin_ref[:, span] = (gout_ref[:, span].astype(F32) + inverse_rms * scaled - part * mean).astype(BF)
     for k, (_, slot) in enumerate(near):
         ga_link.arrived(k, ga0.at[slot], core_dev)
     ga1[z] = (ga0[0] + ga0[1]) + (ga0[2] + ga0[3])
@@ -504,41 +505,54 @@
         ga_link.start(2 + k, ga1.at[z], ga1.at[z], z_dev[k])
 
     gnc.last_pair()
-    ggc.last_pair()
     for k in range(1, 4):
         ga_link.arrived(2 + k, ga1.at[(z + 4 - k) % 4], core_dev)
     ga2[dp] = (ga1[0] + ga1[1]) + (ga1[2] + ga1[3])
     for k in range(1, 8):
         ga_link.start(5 + k, ga2.at[dp], ga2.at[dp], ((dp + k) % 8, head))
 
+    for k in range(1, 8):
+        cols.arrived(6 + k, gc.at[(dp + 8 - k) % 8, :, :, 1 - c], core_dev)
+    total = None
+    for s in range(8):
+        term = dot_tn(att[s // 2, s % 2], gc[s].reshape(SEQ, CHUNK))
+        total = term if total is None else total + term
+    gwo_ref[...] = total.astype(BF)
+    gqk.on_far()
     gnc.done(other_core(nc))
     total = None
     for s in range(8):
         term = dot_tn(nc[s].reshape(SEQ, CHUNK), qkv[s // 2, s % 2])
         total = term if total is None else total + term
     gwq_ref[...] = total[:, : HEADS * HD].astype(BF)
-    gwk_ref[...] = total[:, HEADS * HD : HEADS * HD + HD // 2].astype(BF)
-    gwv_ref[...] = total[:, HEADS * HD + HD // 2 :].astype(BF)
-    ggc.done(other_core(gc))
-    total = None
-    for s in range(8):
-        term = dot_tn(att[s // 2, s % 2], gc[s].reshape(SEQ, CHUNK))
-        total = term if total is None else total + term
-    gwo_ref[...] = total.astype(BF)
+    pairs = total[:, HEADS * HD :].T
+    gwk_ref[...] = pairs[: HD // 2].astype(BF)
+    gwv_ref[...] = pairs[HD // 2 :].astype(BF)
 
     for k in range(1, 8):
         ga_link.arrived(5 + k, ga2.at[(dp + 8 - k) % 8], core_dev)
-    ggain_ref[...] = ((ga2[0] + ga2[1]) + (ga2[2] + ga2[3])) + ((ga2[4] + ga2[5]) + (ga2[6] + ga2[7]))
-
-    for link in (gat, gqk, gnc, ggc, ro, rg, kv_link, ga_link):
+    total = ((ga2[0] + ga2[1]) + (ga2[2] + ga2[3])) + ((ga2[4] + ga2[5]) + (ga2[6] + ga2[7]))
+    for ch in range(CHUNKS):
+        ggain_ref[:, ch * CHUNK : (ch + 1) * CHUNK] = total[ch : ch + 1]
+
+    for link in (gg, gat, gqk, gnc, cols, ro, rg, kv_link, ga_link):
         link.sent()
 
 
+def hand_over(*refs):
+    src, dst, mid, sem_in, sem_out = refs[:7], refs[7:14], refs[14:21], refs[21], refs[22]
+    loads = [pltpu.make_async_copy(src[i], mid[i], sem_in.at[i]) for i in range(7)]
+    stores = [pltpu.make_async_copy(mid[i], dst[i], sem_out.at[i]) for i in range(7)]
+    for cp in loads:
+        cp.start()
+    for load, store in zip(loads, stores):
+        load.wait()
+        store.start()
+    for cp in stores:
+        cp.wait()
+
+
 def per_device(inputs, gain, doc_ids, w_query, w_key, w_value, w_out, grad_out):
-    w_kv = jnp.concatenate([w_key, w_value], axis=1)
-    exponent = jnp.arange(HD // 2, dtype=F32) * (2.0 / HD)
-    frequency = THETA ** (-exponent)
-    frequency = jnp.concatenate([frequency, frequency])[None, :]
     vmem = pl.BlockSpec(memory_space=pltpu.VMEM)
     hbm = pl.BlockSpec(memory_space=pl.ANY)
     rows = (CHUNKS, 2, 4, 2, ROWS, CHUNK)
@@ -557,21 +571,22 @@
         out_shape=(
             jax.ShapeDtypeStruct((ROWS, CHUNKS * CHUNK), BF),
             jax.ShapeDtypeStruct((ROWS, CHUNKS * CHUNK), BF),
-            jax.ShapeDtypeStruct((CHUNKS, CHUNK), F32),
+            jax.ShapeDtypeStruct((1, CHUNKS * CHUNK), F32),
             jax.ShapeDtypeStruct((CHUNK, HEADS * HD), BF),
-            jax.ShapeDtypeStruct((CHUNK, HD // 2), BF),
-            jax.ShapeDtypeStruct((CHUNK, HD // 2), BF),
+            jax.ShapeDtypeStruct((HD // 2, CHUNK), BF),
+            jax.ShapeDtypeStruct((HD // 2, CHUNK), BF),
             jax.ShapeDtypeStruct((HEADS * HD, CHUNK), BF),
         ),
-        in_specs=[vmem] * 5 + [hbm] * 3 + [vmem],
+        in_specs=[vmem] * 3 + [hbm] * 4 + [vmem],
         out_specs=[vmem] * 7,
         scratch_shapes=[
             pltpu.VMEM(rows, BF),
             pltpu.VMEM(rows, BF),
             pltpu.VMEM(rows, BF),
             pltpu.VMEM(rows, BF),
+            pltpu.VMEM(rows, BF),
             pltpu.VMEM((CHUNKS * CHUNK, HEADS * HD), BF),
-            pltpu.VMEM((CHUNKS * CHUNK, HD), BF),
+            pltpu.VMEM((HD, CHUNKS * CHUNK), BF),
             pltpu.VMEM((HEADS * HD, CHUNKS * CHUNK), BF),
             pltpu.VMEM((4, 2, SEQ, HEADS * HD), BF),
             pltpu.VMEM((4, 2, SEQ, HEADS * HD + HD), BF),
@@ -582,7 +597,7 @@
             pltpu.VMEM((HEADS, SEQ, SEQ), F32),
         ]
         + scatter
-        + scatter
+        + scatter[1:]
         + [
             pltpu.VMEM((4, CHUNKS, CHUNK), F32),
             pltpu.VMEM((4, CHUNKS, CHUNK), F32),
@@ -591,10 +606,10 @@
         + dma(17) * 4
         + dma(9) * 2
         + dma(16) * 2
-        + dma(7) * 2
+        + dma(7)
         + dma(2)
         + dma(13)
-        + [pltpu.SemaphoreType.DMA((3,))],
+        + [pltpu.SemaphoreType.DMA((4,))],
         compiler_params=pltpu.CompilerParams(
             collective_id=0, has_side_effects=True, vmem_limit_bytes=60 * 2**20
         ),
@@ -602,15 +617,20 @@
         inputs,
         gain[None, :],
         doc_ids,
-        doc_ids.reshape(SEQ, 1),
-        frequency,
         w_query,
-        w_kv,
+        w_key.T,
+        w_value.T,
         w_out,
         grad_out,
     )
-    out, gin, ggain, gwq, gwk, gwv, gwo = outs
-    return (out, gin, ggain.reshape(-1), gwq, gwk, gwv, gwo)
+    out, gin, ggain, gwq, gwk, gwv, gwo = pl.pallas_call(
+        hand_over,
+        out_shape=[jax.ShapeDtypeStruct(o.shape, o.dtype) for o in outs],
+        in_specs=[hbm] * 7,
+        out_specs=[hbm] * 7,
+        scratch_shapes=[pltpu.VMEM(o.shape, o.dtype) for o in outs] + dma(7),
+    )(*outs)
+    return (out, gin, ggain.reshape(-1), gwq, gwk.T, gwv.T, gwo)
 
 
 def solution(mesh):

time: 182 us -> 147 us (0.81)
  local copies, waits for them, and re-layouts: 16.2 us -> 0 us
  Pallas kernels: 159 us -> 146 us
  other arithmetic: 4.69 us -> 0 us
    pallas_call x1, Pallas kernels: 159 us -> 143 us  [per_device(): pl.pallas_call(layer, out_shape=(jax.ShapeDtypeStruct((ROWS, CHUNKS * CHU...]
    unnamed x15 -> x0, local copies, waits for them, and re-layouts: 15.4 us -> none
    concatenate x1 -> x0, other arithmetic: 4.08 us -> none  [per_device(): w_kv = jnp.concatenate([w_key, w_value], axis=1)]
    pallas_call x0 -> x1, Pallas kernels: none -> 2.94 us  [per_device(): pl.pallas_call(hand_over, out_shape=[jax.ShapeDtypeStruct(o.shape, o.dtyp...]
where the time goes in v2:
time: 147 us
  Pallas kernels  146 us (99%)
    pallas_call x1, Pallas kernels, per_device(): pl.pallas_call(layer, out_shape=(jax.ShapeDtypeStruct((ROWS, CHUNKS * CHU...  143 us

profile of v2, /device:TPU:1, one launch (start us, length us, event | category | flops | bytes accessed | tf_op | source)
XLA Modules:
  0.0 146.7 jit_solution(12684750980940695245)
XLA Ops:
  0.6 143.1 %shard_map.135 = (bf16[16,8192]{1,0:T(8,128)(2,1)}, bf16[16,8192]{1,0:T(8,128)(2,1)}, f32[1,8192]{1,0:T(1,128)}, bf16[1024,512]{1,0:T(8,128)(2,1)}, bf16[64,1024...) custom-call(bf16[16,8192]{1,0:T(8,128)(2,1)} %inputs_ref.1, f32[1,8192]{1,0:T(1,128)} %bitcast.8, ...), custom_call_target="tpu_custom_call" | custom-call | tf_op jit(solution)/shard_map/pallas_call | solution.py:569
  143.8 2.9 %shard_map.136 = (bf16[16,8192]{1,0:T(8,128)(2,1)}, bf16[16,8192]{1,0:T(8,128)(2,1)}, f32[1,8192]{1,0:T(1,128)}, bf16[1024,512]{1,0:T(8,128)(2,1)}, bf16[64,1024...) custom-call(bf16[16,8192]{1,0:T(8,128)(2,1)} %get-tuple-element.21.refs_0_, ...), custom_call_target="tpu_custom_call" | custom-call | tf_op jit(solution)/shard_map/pallas_call | solution.py:626

commit v3 on v2

--- a/solution.py
+++ b/solution.py
@@ -238,7 +238,7 @@
 def layer(
     inputs_ref, gain_ref, doc_ref, wq_hbm, wk_hbm, wv_hbm, wo_hbm, gout_ref,
     out_ref, gin_ref, ggain_ref, gwq_ref, gwk_ref, gwv_ref, gwo_ref,
-    xs, gs, nc, gc, pg, wq, wkv, wo, att, qkv, acc, kvh, kvg, qh, probs,
+    xs, gs, nc, gc, po, wq, wkv, wo, att, qkv, acc, kvh, kvg, qh, probs,
     rs0, rs1, rs2, rs3, rs4, rs5, rt1, rt2, rt3, rt4, rt5,
     ga0, ga1, ga2,
     x_s, x_r, g_s, g_r, nc_s, nc_r, gc_s, gc_r, at_s, at_r, qk_s, qk_r, ro_s, ro_r, rg_s, rg_r,
@@ -279,7 +279,7 @@
         part = inputs_ref[:, cols].astype(F32)
         xs[ch, yl, z, c] = (part * inverse_rms * gain_ref[:, cols]).astype(BF)
         gs[ch, yl, z, c] = gout_ref[:, cols]
-    nc[dp, yl, z, c] = xs[dp, yl, z, c]
+    gc[dp, yl, z, c] = gs[dp, yl, z, c]
 
     pl.semaphore_wait(barrier, len(partners))
 
@@ -303,20 +303,19 @@
         )
 
     gx, gg = head_gather(xs, x_s, x_r), head_gather(gs, g_s, g_r)
-    gnc = head_gather(nc, nc_s, nc_r)
-    cols = Link(gc_s, gc_r)
+    ggc = head_gather(gc, gc_s, gc_r)
+    cols = Link(nc_s, nc_r)
     gat, gqk = dp_gather(att, at_s, at_r), dp_gather(qkv, qk_s, qk_r)
     devs = (core_dev, pair_dev, z_dev[1], z_dev[3])
-    ro = Scatter(Link(ro_s, ro_r), xs, (rs0, rs1, rs2, rs3, rs4, rs5), (yl, z, c), devs)
-    rg = Scatter(Link(rg_s, rg_r), pg, (rs0, rt1, rt2, rt3, rt4, rt5), (yl, z, c), devs)
+    ro = Scatter(Link(ro_s, ro_r), po, (rs0, rs1, rs2, rs3, rs4, rs5), (yl, z, c), devs)
+    rg = Scatter(Link(rg_s, rg_r), gs, (rs0, rt1, rt2, rt3, rt4, rt5), (yl, z, c), devs)
 
     gx.start_ring()
     gx.start_pair()
-    gg.start_pair()
     tiny = Link(tn_s, tn_r)
     for k in range(1, 8):
         to = (dp + k) % 8
-        tiny.start(k - 1, xs.at[to, yl, z, c], nc.at[dp, yl, z, c], (to, head))
+        tiny.start(k - 1, gs.at[to, yl, z, c], gc.at[dp, yl, z, c], (to, head))
 
     row_index = lax.broadcasted_iota(jnp.int32, (SEQ, SEQ), 0)
     col_index = lax.broadcasted_iota(jnp.int32, (SEQ, SEQ), 1)
@@ -339,12 +338,18 @@
         return g * cosine + jnp.where(low_half, turned, -turned)
 
     gx.on_pair()
+    gg.start_pair()
     gx.on_ring_own()
     gx.on_ring_pair()
     gg.start_ring()
     gg.on_pair()
     gx.on_far()
     gx.done(other_core(xs))
+
+    for k in range(1, 8):
+        to = (dp + k) % 8
+        cols.start(k - 1, xs.at[to, :, :, c], nc.at[dp, :, :, c], (to, head))
+    nc[dp] = xs[dp]
 
     for cp in weights[:3]:
         cp.wait()
@@ -386,31 +391,25 @@
     gat.start_pair()
     gg.on_ring_pair()
 
-    gx.sent()
-    tiny.sent()
     weights[3].wait()
     wide = (2, 4, 2, ROWS, CHUNK)
 
     def project_out(ch, carry):
         cols_ch = pl.ds(pl.multiple_of(ch * CHUNK, CHUNK), CHUNK)
-        xs[ch] = dot(att[x, yh], wo[:, cols_ch]).astype(BF).reshape(wide)
+        po[ch] = dot(att[x, yh], wo[:, cols_ch]).astype(BF).reshape(wide)
         ro.give_core(ch)
         return carry
 
     lax.fori_loop(0, CHUNKS, project_out, 0)
     ro.add_core()
     gg.on_far()
+    for k in range(1, 8):
+        tiny.arrived(k - 1, gc.at[(dp + 8 - k) % 8, yl, z, c], core_dev)
+    ggc.start_ring()
+    ggc.start_pair()
     ro.start()
     gat.on_pair()
     gg.done(other_core(gs))
-
-    for k in range(1, 8):
-        to = (dp + k) % 8
-        cols.start(k - 1, gs.at[to, :, :, c], gc.at[dp, :, :, c], (to, head))
-    gc[dp] = gs[dp]
-    for k in range(1, 8):
-        tiny.arrived(k - 1, nc.at[(dp + 8 - k) % 8, yl, z, c], core_dev)
-    gnc.start_pair()
 
     acc[...] = jnp.zeros_like(acc)
 
@@ -421,6 +420,7 @@
 
     lax.fori_loop(0, CHUNKS, back_out, 0)
     gat.on_ring_own()
+    ggc.on_pair()
     key_sum = jnp.zeros((SEQ, HD), F32)
     value_sum = jnp.zeros((SEQ, HD), F32)
     for h in range(HEADS):
@@ -446,80 +446,62 @@
     gqk.start_ring()
     gqk.start_pair()
     gat.on_ring_pair()
+    ggc.on_ring_own()
+    gg.sent()
+    tiny.sent()
 
     def back_in(ch, carry):
         rows = pl.ds(pl.multiple_of(ch * CHUNK, CHUNK), CHUNK)
         part = dot_nt(qkv[x, yh, :, : HEADS * HD], wq[rows, :])
         part += dot(qkv[x, yh, :, HEADS * HD :], wkv[:, rows])
-        pg[ch] = part.astype(BF).reshape(wide)
+        gs[ch] = part.astype(BF).reshape(wide)
         rg.give_core(ch)
         return carry
 
     lax.fori_loop(0, CHUNKS, back_in, 0)
     rg.add_core()
     rg.start()
-    gnc.start_ring()
+
+    gain_slot = yl * 2 + c
+    for ch in range(CHUNKS):
+        term = gs[ch, :, :, c].astype(F32) * xs[ch, :, :, c].astype(F32)
+        term = jnp.sum(term.reshape(SEQ // 2, CHUNK), axis=0, keepdims=True)
+        ga0[gain_slot, ch : ch + 1] = term / gain_ref[:, ch * CHUNK : (ch + 1) * CHUNK]
+    ga_link = Link(ga_s, ga_r)
+    near = [(core_dev, yl * 2 + 1 - c), (pair_dev, (1 - yl) * 2 + c), (diag_dev, (1 - yl) * 2 + 1 - c)]
+    for k, (to, _) in enumerate(near):
+        ga_link.start(k, ga0.at[gain_slot], ga0.at[gain_slot], to)
+
     gqk.on_pair()
     ro.to_pair()
+    for k in range(1, 8):
+        block = nc.at[(dp + 8 - k) % 8, :, :, c]
+        cols.arrived(k - 1, block, core_dev)
+        cols.start(6 + k, block, block, core_dev)
+    for k, (_, slot) in enumerate(near):
+        ga_link.arrived(k, ga0.at[slot], core_dev)
+    ga1[z] = (ga0[0] + ga0[1]) + (ga0[2] + ga0[3])
+    for k in range(1, 4):
+        ga_link.start(2 + k, ga1.at[z], ga1.at[z], z_dev[k])
     gat.on_far()
     gqk.on_ring_own()
     rg.middle()
+    ggc.on_ring_pair()
     for h in range(2):
         ro.arrived(h)
         for ch in range(4 * h, 4 * h + 4):
             span = slice(ch * CHUNK, (ch + 1) * CHUNK)
             out_ref[:, span] = (inputs_ref[:, span].astype(F32) + ro.chunk(ch)).astype(BF)
     gqk.on_ring_pair()
-    gnc.last_ring()
-    for k in range(1, 8):
-        block = gc.at[(dp + 8 - k) % 8, :, :, c]
-        cols.arrived(k - 1, block, core_dev)
-        cols.start(6 + k, block, block, core_dev)
-    rg.to_pair()
-    gnc.last_far()
-
-    mean = jnp.zeros((ROWS, 1), F32)
-    gain_slot = yl * 2 + c
-    for h in range(2):
-        rg.arrived(h)
-        for ch in range(4 * h, 4 * h + 4):
-            span = slice(ch * CHUNK, (ch + 1) * CHUNK)
-            grad = rg.chunk(ch)
-            part = inputs_ref[:, span].astype(F32)
-            ga0[gain_slot, ch : ch + 1] = jnp.sum(grad * part * inverse_rms, axis=0, keepdims=True)
-            mean += jnp.sum(grad * gain_ref[:, span] * part, axis=-1, keepdims=True)
-    ga_link = Link(ga_s, ga_r)
-    near = [(core_dev, yl * 2 + 1 - c), (pair_dev, (1 - yl) * 2 + c), (diag_dev, (1 - yl) * 2 + 1 - c)]
-    for k, (to, _) in enumerate(near):
-        ga_link.start(k, ga0.at[gain_slot], ga0.at[gain_slot], to)
-    mean = mean * (1.0 / (CHUNKS * CHUNK)) * inverse_rms * inverse_rms * inverse_rms
-    for ch in range(CHUNKS):
-        span = slice(ch * CHUNK, (ch + 1) * CHUNK)
-        part = inputs_ref[:, span].astype(F32)
-        scaled = rg.chunk(ch) * gain_ref[:, span]
-        gin_ref[:, span] = (gout_ref[:, span].astype(F32) + inverse_rms * scaled - part * mean).astype(BF)
-    for k, (_, slot) in enumerate(near):
-        ga_link.arrived(k, ga0.at[slot], core_dev)
-    ga1[z] = (ga0[0] + ga0[1]) + (ga0[2] + ga0[3])
-    for k in range(1, 4):
-        ga_link.start(2 + k, ga1.at[z], ga1.at[z], z_dev[k])
-
-    gnc.last_pair()
     for k in range(1, 4):
         ga_link.arrived(2 + k, ga1.at[(z + 4 - k) % 4], core_dev)
     ga2[dp] = (ga1[0] + ga1[1]) + (ga1[2] + ga1[3])
     for k in range(1, 8):
         ga_link.start(5 + k, ga2.at[dp], ga2.at[dp], ((dp + k) % 8, head))
-
     for k in range(1, 8):
-        cols.arrived(6 + k, gc.at[(dp + 8 - k) % 8, :, :, 1 - c], core_dev)
-    total = None
-    for s in range(8):
-        term = dot_tn(att[s // 2, s % 2], gc[s].reshape(SEQ, CHUNK))
-        total = term if total is None else total + term
-    gwo_ref[...] = total.astype(BF)
+        cols.arrived(6 + k, nc.at[(dp + 8 - k) % 8, :, :, 1 - c], core_dev)
+
     gqk.on_far()
-    gnc.done(other_core(nc))
     total = None
     for s in range(8):
         term = dot_tn(nc[s].reshape(SEQ, CHUNK), qkv[s // 2, s % 2])
@@ -528,14 +510,34 @@
     pairs = total[:, HEADS * HD :].T
     gwk_ref[...] = pairs[: HD // 2].astype(BF)
     gwv_ref[...] = pairs[HD // 2 :].astype(BF)
-
+    rg.to_pair()
+    ggc.on_far()
     for k in range(1, 8):
         ga_link.arrived(5 + k, ga2.at[(dp + 8 - k) % 8], core_dev)
     total = ((ga2[0] + ga2[1]) + (ga2[2] + ga2[3])) + ((ga2[4] + ga2[5]) + (ga2[6] + ga2[7]))
     for ch in range(CHUNKS):
         ggain_ref[:, ch * CHUNK : (ch + 1) * CHUNK] = total[ch : ch + 1]
-
-    for link in (gg, gat, gqk, gnc, cols, ro, rg, kv_link, ga_link):
+    mean = jnp.zeros((ROWS, 1), F32)
+    for h in range(2):
+        rg.arrived(h)
+        for ch in range(4 * h, 4 * h + 4):
+            span = slice(ch * CHUNK, (ch + 1) * CHUNK)
+            part = inputs_ref[:, span].astype(F32)
+            mean += jnp.sum(rg.chunk(ch) * gain_ref[:, span] * part, axis=-1, keepdims=True)
+    mean = mean * (1.0 / (CHUNKS * CHUNK)) * inverse_rms * inverse_rms * inverse_rms
+    for ch in range(CHUNKS):
+        span = slice(ch * CHUNK, (ch + 1) * CHUNK)
+        part = inputs_ref[:, span].astype(F32)
+        scaled = rg.chunk(ch) * gain_ref[:, span]
+        gin_ref[:, span] = (gout_ref[:, span].astype(F32) + inverse_rms * scaled - part * mean).astype(BF)
+    ggc.done(other_core(gc))
+    total = None
+    for s in range(8):
+        term = dot_tn(att[s // 2, s % 2], gc[s].reshape(SEQ, CHUNK))
+        total = term if total is None else total + term
+    gwo_ref[...] = total.astype(BF)
+
+    for link in (gx, gat, gqk, ggc, cols, ro, rg, kv_link, ga_link):
         link.sent()
 
 

time: 147 us -> 131 us (0.89)
  the two profiles are of different devices: /device:TPU:1 before, /device:TPU:19 now
where the time goes in v3:
time: 131 us
  Pallas kernels  130 us (99%)
    pallas_call x1, Pallas kernels, per_device(): pl.pallas_call(layer, out_shape=(jax.ShapeDtypeStruct((ROWS, CHUNKS * CHU...  127 us
    pallas_call x1, Pallas kernels, per_device(): pl.pallas_call(hand_over, out_shape=[jax.ShapeDtypeStruct(o.shape, o.dtyp...  2.94 us

profile of v3, /device:TPU:19, one launch (start us, length us, event | category | flops | bytes accessed | tf_op | source)
XLA Modules:
  0.0 130.7 jit_solution(5173169010091305697)
XLA Ops:
  0.6 126.9 %shard_map.135 = (bf16[16,8192]{1,0:T(8,128)(2,1)}, bf16[16,8192]{1,0:T(8,128)(2,1)}, f32[1,8192]{1,0:T(1,128)}, bf16[1024,512]{1,0:T(8,128)(2,1)}, bf16[64,1024...) custom-call(bf16[16,8192]{1,0:T(8,128)(2,1)} %inputs_ref.1, f32[1,8192]{1,0:T(1,128)} %bitcast.8, ...), custom_call_target="tpu_custom_call" | custom-call | tf_op jit(solution)/shard_map/pallas_call | solution.py:571
  127.6 2.9 %shard_map.136 = (bf16[16,8192]{1,0:T(8,128)(2,1)}, bf16[16,8192]{1,0:T(8,128)(2,1)}, f32[1,8192]{1,0:T(1,128)}, bf16[1024,512]{1,0:T(8,128)(2,1)}, bf16[64,1024...) custom-call(bf16[16,8192]{1,0:T(8,128)(2,1)} %get-tuple-element.21.refs_0_, ...), custom_call_target="tpu_custom_call" | custom-call | tf_op jit(solution)/shard_map/pallas_call | solution.py:628

commit v4 on v3

--- a/solution.py
+++ b/solution.py
@@ -17,6 +17,7 @@
 CHUNKS = 8
 CHUNK = 1024
 SEQ = 256
+CUT = 512
 HEADS = 4
 HD = 128
 
@@ -238,10 +239,10 @@
 def layer(
     inputs_ref, gain_ref, doc_ref, wq_hbm, wk_hbm, wv_hbm, wo_hbm, gout_ref,
     out_ref, gin_ref, ggain_ref, gwq_ref, gwk_ref, gwv_ref, gwo_ref,
-    xs, gs, nc, gc, po, wq, wkv, wo, att, qkv, acc, kvh, kvg, qh, probs,
+    xs, gs, nc, gc, po, ms, wq, wkv, wo, att, qkv, acc, kvh, kvg, qh, probs,
     rs0, rs1, rs2, rs3, rs4, rs5, rt1, rt2, rt3, rt4, rt5,
     ga0, ga1, ga2,
-    x_s, x_r, g_s, g_r, nc_s, nc_r, gc_s, gc_r, at_s, at_r, qk_s, qk_r, ro_s, ro_r, rg_s, rg_r,
+    x_s, x_r, g_s, g_r, nc_s, nc_r, gc_s, gc_r, fc_s, fc_r, at_s, at_r, qk_s, qk_r, ro_s, ro_r, rg_s, rg_r,
     tn_s, tn_r, kv_s, kv_r, ga_s, ga_r, w_sem,
 ):
     dp, head = lax.axis_index("dp"), lax.axis_index("head")
@@ -303,8 +304,10 @@
         )
 
     gx, gg = head_gather(xs, x_s, x_r), head_gather(gs, g_s, g_r)
-    ggc = head_gather(gc, gc_s, gc_r)
+    near_cols = gc.at[:, :, :, :, :, 0:CUT]
+    ggc = head_gather(near_cols, gc_s, gc_r)
     cols = Link(nc_s, nc_r)
+    far_cols = Link(fc_s, fc_r)
     gat, gqk = dp_gather(att, at_s, at_r), dp_gather(qkv, qk_s, qk_r)
     devs = (core_dev, pair_dev, z_dev[1], z_dev[3])
     ro = Scatter(Link(ro_s, ro_r), po, (rs0, rs1, rs2, rs3, rs4, rs5), (yl, z, c), devs)
@@ -315,7 +318,7 @@
     tiny = Link(tn_s, tn_r)
     for k in range(1, 8):
         to = (dp + k) % 8
-        tiny.start(k - 1, gs.at[to, yl, z, c], gc.at[dp, yl, z, c], (to, head))
+        tiny.start(k - 1, gs.at[to, yl, z, c, :, 0:CUT], gc.at[dp, yl, z, c, :, 0:CUT], (to, head))
 
     row_index = lax.broadcasted_iota(jnp.int32, (SEQ, SEQ), 0)
     col_index = lax.broadcasted_iota(jnp.int32, (SEQ, SEQ), 1)
@@ -337,18 +340,58 @@
         turned = pltpu.roll(g * sine, HD // 2, 1)
         return g * cosine + jnp.where(low_half, turned, -turned)
 
+    spots = [
+        (yl, z), (1 - yl, z), (yl, gx.prv), (yl, gx.nxt),
+        (1 - yl, gx.prv), (1 - yl, gx.nxt), (yl, gx.far), (1 - yl, gx.far),
+    ]
+
+    def spread_copy(i, k):
+        p, r = spots[i]
+        to = (dp + k) % 8
+        return cols.copy(7 * i + k - 1, xs.at[to, p, r, c], nc.at[dp, p, r, c], (to, head))
+
+    def spread(*blocks):
+        def step(k, carry):
+            for i in blocks:
+                spread_copy(i, k).start()
+            return carry
+
+        lax.fori_loop(1, 8, step, 0)
+
+    def spread_share(k):
+        block = nc.at[(dp + 8 - k) % 8, :, :, c]
+        return cols.copy(55 + k, block, block, core_dev)
+
+    def collect(k, carry):
+        for i in range(8):
+            p, r = spots[i]
+            cols.arrived(7 * i + k - 1, nc.at[(dp + 8 - k) % 8, p, r, c], core_dev)
+        spread_share(k).start()
+        return carry
+
+    def collected(k, carry):
+        cols.arrived(55 + k, nc.at[(dp + 8 - k) % 8, :, :, 1 - c], core_dev)
+        return carry
+
+    def spread_sent(k, carry):
+        for i in range(8):
+            spread_copy(i, k).wait_send()
+        spread_share(k).wait_send()
+        return carry
+
+    spread(0)
     gx.on_pair()
     gg.start_pair()
+    spread(1)
     gx.on_ring_own()
+    spread(2, 3)
     gx.on_ring_pair()
+    spread(4, 5)
     gg.start_ring()
     gg.on_pair()
     gx.on_far()
+    spread(6, 7)
     gx.done(other_core(xs))
-
-    for k in range(1, 8):
-        to = (dp + k) % 8
-        cols.start(k - 1, xs.at[to, :, :, c], nc.at[dp, :, :, c], (to, head))
     nc[dp] = xs[dp]
 
     for cp in weights[:3]:
@@ -404,12 +447,19 @@
     ro.add_core()
     gg.on_far()
     for k in range(1, 8):
-        tiny.arrived(k - 1, gc.at[(dp + 8 - k) % 8, yl, z, c], core_dev)
+        tiny.arrived(k - 1, gc.at[(dp + 8 - k) % 8, yl, z, c, :, 0:CUT], core_dev)
     ggc.start_ring()
     ggc.start_pair()
     ro.start()
     gat.on_pair()
     gg.done(other_core(gs))
+    for ch in range(CHUNKS):
+        ms[ch] = gs[ch, :, :, c, :, CUT:]
+    for k in range(1, 8):
+        to = (dp + k) % 8
+        far_cols.start(k - 1, ms.at[to], gc.at[dp, :, :, c, :, CUT:], (to, head))
+    gc[dp, :, :, :, :, CUT:] = gs[dp, :, :, :, :, CUT:]
+    lax.fori_loop(1, 8, collect, 0)
 
     acc[...] = jnp.zeros_like(acc)
 
@@ -473,18 +523,14 @@
         ga_link.start(k, ga0.at[gain_slot], ga0.at[gain_slot], to)
 
     gqk.on_pair()
+    gqk.on_ring_own()
     ro.to_pair()
-    for k in range(1, 8):
-        block = nc.at[(dp + 8 - k) % 8, :, :, c]
-        cols.arrived(k - 1, block, core_dev)
-        cols.start(6 + k, block, block, core_dev)
     for k, (_, slot) in enumerate(near):
         ga_link.arrived(k, ga0.at[slot], core_dev)
     ga1[z] = (ga0[0] + ga0[1]) + (ga0[2] + ga0[3])
     for k in range(1, 4):
         ga_link.start(2 + k, ga1.at[z], ga1.at[z], z_dev[k])
     gat.on_far()
-    gqk.on_ring_own()
     rg.middle()
     ggc.on_ring_pair()
     for h in range(2):
@@ -493,14 +539,18 @@
             span = slice(ch * CHUNK, (ch + 1) * CHUNK)
             out_ref[:, span] = (inputs_ref[:, span].astype(F32) + ro.chunk(ch)).astype(BF)
     gqk.on_ring_pair()
+    for k in range(1, 8):
+        block = gc.at[(dp + 8 - k) % 8, :, :, c, :, CUT:]
+        far_cols.arrived(k - 1, block, core_dev)
+        far_cols.start(6 + k, block, block, core_dev)
     for k in range(1, 4):
         ga_link.arrived(2 + k, ga1.at[(z + 4 - k) % 4], core_dev)
     ga2[dp] = (ga1[0] + ga1[1]) + (ga1[2] + ga1[3])
     for k in range(1, 8):
         ga_link.start(5 + k, ga2.at[dp], ga2.at[dp], ((dp + k) % 8, head))
-    for k in range(1, 8):
-        cols.arrived(6 + k, nc.at[(dp + 8 - k) % 8, :, :, 1 - c], core_dev)
-
+
+    lax.fori_loop(1, 8, collected, 0)
+    rg.to_pair()
     gqk.on_far()
     total = None
     for s in range(8):
@@ -510,7 +560,6 @@
     pairs = total[:, HEADS * HD :].T
     gwk_ref[...] = pairs[: HD // 2].astype(BF)
     gwv_ref[...] = pairs[HD // 2 :].astype(BF)
-    rg.to_pair()
     ggc.on_far()
     for k in range(1, 8):
         ga_link.arrived(5 + k, ga2.at[(dp + 8 - k) % 8], core_dev)
@@ -530,14 +579,17 @@
         part = inputs_ref[:, span].astype(F32)
         scaled = rg.chunk(ch) * gain_ref[:, span]
         gin_ref[:, span] = (gout_ref[:, span].astype(F32) + inverse_rms * scaled - part * mean).astype(BF)
-    ggc.done(other_core(gc))
+    ggc.done(other_core(near_cols))
+    for k in range(1, 8):
+        far_cols.arrived(6 + k, gc.at[(dp + 8 - k) % 8, :, :, 1 - c, :, CUT:], core_dev)
     total = None
     for s in range(8):
         term = dot_tn(att[s // 2, s % 2], gc[s].reshape(SEQ, CHUNK))
         total = term if total is None else total + term
     gwo_ref[...] = total.astype(BF)
 
-    for link in (gx, gat, gqk, ggc, cols, ro, rg, kv_link, ga_link):
+    lax.fori_loop(1, 8, spread_sent, 0)
+    for link in (gx, gat, gqk, ggc, far_cols, ro, rg, kv_link, ga_link):
         link.sent()
 
 
@@ -587,6 +639,7 @@
             pltpu.VMEM(rows, BF),
             pltpu.VMEM(rows, BF),
             pltpu.VMEM(rows, BF),
+            pltpu.VMEM((CHUNKS, 2, 4, ROWS, CHUNK - CUT), BF),
             pltpu.VMEM((CHUNKS * CHUNK, HEADS * HD), BF),
             pltpu.VMEM((HD, CHUNKS * CHUNK), BF),
             pltpu.VMEM((HEADS * HD, CHUNKS * CHUNK), BF),
@@ -605,7 +658,10 @@
             pltpu.VMEM((4, CHUNKS, CHUNK), F32),
             pltpu.VMEM((8, CHUNKS, CHUNK), F32),
         ]
-        + dma(17) * 4
+        + dma(17) * 2
+        + dma(63)
+        + dma(17)
+        + dma(14)
         + dma(9) * 2
         + dma(16) * 2
         + dma(7)
@@ -613,7 +669,7 @@
         + dma(13)
         + [pltpu.SemaphoreType.DMA((4,))],
         compiler_params=pltpu.CompilerParams(
-            collective_id=0, has_side_effects=True, vmem_limit_bytes=60 * 2**20
+            collective_id=0, has_side_effects=True, vmem_limit_bytes=62 * 2**20
         ),
     )(
         inputs,

time: 131 us -> 122 us (0.931)
  the two profiles are of different devices: /device:TPU:19 before, /device:TPU:1 now
where the time goes in v4:
time: 122 us
  Pallas kernels  121 us (99%)
    pallas_call x1, Pallas kernels, per_device(): pl.pallas_call(layer, out_shape=(jax.ShapeDtypeStruct((ROWS, CHUNKS * CHU...  118 us
    pallas_call x1, Pallas kernels, per_device(): pl.pallas_call(hand_over, out_shape=[jax.ShapeDtypeStruct(o.shape, o.dtyp...  2.94 us

profile of v4, /device:TPU:1, one launch (start us, length us, event | category | flops | bytes accessed | tf_op | source)
XLA Modules:
  0.0 122.2 jit_solution(16606592044491732396)
XLA Ops:
  0.6 118.5 %shard_map.135 = (bf16[16,8192]{1,0:T(8,128)(2,1)}, bf16[16,8192]{1,0:T(8,128)(2,1)}, f32[1,8192]{1,0:T(1,128)}, bf16[1024,512]{1,0:T(8,128)(2,1)}, bf16[64,1024...) custom-call(bf16[16,8192]{1,0:T(8,128)(2,1)} %inputs_ref.1, f32[1,8192]{1,0:T(1,128)} %bitcast.8, ...), custom_call_target="tpu_custom_call" | custom-call | tf_op jit(solution)/shard_map/pallas_call | solution.py:623
  119.1 2.9 %shard_map.136 = (bf16[16,8192]{1,0:T(8,128)(2,1)}, bf16[16,8192]{1,0:T(8,128)(2,1)}, f32[1,8192]{1,0:T(1,128)}, bf16[1024,512]{1,0:T(8,128)(2,1)}, bf16[64,1024...) custom-call(bf16[16,8192]{1,0:T(8,128)(2,1)} %get-tuple-element.21.refs_0_, ...), custom_call_target="tpu_custom_call" | custom-call | tf_op jit(solution)/shard_map/pallas_call | solution.py:684

commit v5 on v4

--- a/solution.py
+++ b/solution.py
@@ -17,7 +17,7 @@
 CHUNKS = 8
 CHUNK = 1024
 SEQ = 256
-CUT = 512
+CUT = 768
 HEADS = 4
 HD = 128
 
@@ -171,26 +171,47 @@
             ch, self.parts.at[ch, :, :, 1 - self.c], self.from_core.at[ch], self.core_dev
         ).start()
 
-    def add_core(self):
-        def step(ch, carry):
-            self.link.copy(
-                ch, self.parts.at[ch, :, :, 1 - self.c], self.from_core.at[ch], self.core_dev
-            ).wait()
-            own = self.parts[ch, :, :, self.c].astype(F32)
-            self.parts[ch, :, :, self.c] = (own + self.from_core[ch].astype(F32)).astype(BF)
+    def add_core(self, ch):
+        self.link.copy(
+            ch, self.parts.at[ch, :, :, 1 - self.c], self.from_core.at[ch], self.core_dev
+        ).wait()
+        own = self.parts[ch, :, :, self.c].astype(F32)
+        self.parts[ch, :, :, self.c] = (own + self.from_core[ch].astype(F32)).astype(BF)
+
+    def run(self, make):
+        half = CHUNKS // 2
+
+        def first(ch, carry):
+            make(ch)
             return carry
 
-        lax.fori_loop(0, CHUNKS, step, 0)
+        def second(ch, carry):
+            make(ch)
+            self.add_core(ch - half)
+            return carry
+
+        def rest(ch, carry):
+            self.add_core(ch)
+            return carry
+
+        lax.fori_loop(0, half, first, 0)
+        lax.fori_loop(half, CHUNKS, second, 0)
+        self.start_low()
+        lax.fori_loop(half, CHUNKS, rest, 0)
+        self.start_high()
 
     def half(self, z, h):
         return self.parts.at[4 * h : 4 * h + 4, :, z, self.c]
 
-    def start(self):
+    def start_low(self):
         link = self.link
         link.start(8, self.half(self.far, 0), self.from_prev_half, self.next_dev)
+        link.start(11, self.half(self.prv, 0), self.from_next.at[0:4], self.prev_dev)
+
+    def start_high(self):
+        link = self.link
         link.start(9, self.half(self.far, 1), self.from_next_half, self.prev_dev)
         link.start(10, self.half(self.nxt, 1), self.from_prev.at[4:8], self.next_dev)
-        link.start(11, self.half(self.prv, 0), self.from_next.at[0:4], self.prev_dev)
 
     def middle(self):
         link = self.link
@@ -340,59 +361,44 @@
         turned = pltpu.roll(g * sine, HD // 2, 1)
         return g * cosine + jnp.where(low_half, turned, -turned)
 
-    spots = [
-        (yl, z), (1 - yl, z), (yl, gx.prv), (yl, gx.nxt),
-        (1 - yl, gx.prv), (1 - yl, gx.nxt), (yl, gx.far), (1 - yl, gx.far),
-    ]
-
-    def spread_copy(i, k):
-        p, r = spots[i]
-        to = (dp + k) % 8
-        return cols.copy(7 * i + k - 1, xs.at[to, p, r, c], nc.at[dp, p, r, c], (to, head))
-
-    def spread(*blocks):
+    def spread(*places):
         def step(k, carry):
-            for i in blocks:
-                spread_copy(i, k).start()
+            to = (dp + k) % 8
+            for r in places:
+                cols.copy(k - 1, xs.at[to, :, r, c], nc.at[dp, :, r, c], (to, head)).start()
             return carry
 
         lax.fori_loop(1, 8, step, 0)
 
     def spread_share(k):
         block = nc.at[(dp + 8 - k) % 8, :, :, c]
-        return cols.copy(55 + k, block, block, core_dev)
+        return cols.copy(6 + k, block, block, core_dev)
 
     def collect(k, carry):
-        for i in range(8):
-            p, r = spots[i]
-            cols.arrived(7 * i + k - 1, nc.at[(dp + 8 - k) % 8, p, r, c], core_dev)
+        cols.arrived(k - 1, nc.at[(dp + 8 - k) % 8, :, :, c], core_dev)
         spread_share(k).start()
         return carry
 
     def collected(k, carry):
-        cols.arrived(55 + k, nc.at[(dp + 8 - k) % 8, :, :, 1 - c], core_dev)
+        cols.arrived(6 + k, nc.at[(dp + 8 - k) % 8, :, :, 1 - c], core_dev)
         return carry
 
     def spread_sent(k, carry):
-        for i in range(8):
-            spread_copy(i, k).wait_send()
+        to = (dp + k) % 8
+        cols.copy(k - 1, xs.at[to, :, :, c], nc.at[dp, :, :, c], (to, head)).wait_send()
         spread_share(k).wait_send()
         return carry
 
-    spread(0)
     gx.on_pair()
     gg.start_pair()
-    spread(1)
+    spread(z)
     gx.on_ring_own()
-    spread(2, 3)
     gx.on_ring_pair()
-    spread(4, 5)
     gg.start_ring()
     gg.on_pair()
+    spread(gx.prv, gx.nxt)
     gx.on_far()
-    spread(6, 7)
     gx.done(other_core(xs))
-    nc[dp] = xs[dp]
 
     for cp in weights[:3]:
         cp.wait()
@@ -411,6 +417,7 @@
     kvh[c] = kvh_acc[...].astype(BF)
     kv_link = Link(kv_s, kv_r)
     kv_link.start(0, kvh.at[c], kvh.at[c], core_dev)
+    spread(gx.far)
     gg.on_ring_own()
     for h in range(HEADS):
         pre = acc[:, h * HD : (h + 1) * HD].astype(BF).astype(F32)
@@ -437,38 +444,34 @@
     weights[3].wait()
     wide = (2, 4, 2, ROWS, CHUNK)
 
-    def project_out(ch, carry):
+    def project_out(ch):
         cols_ch = pl.ds(pl.multiple_of(ch * CHUNK, CHUNK), CHUNK)
         po[ch] = dot(att[x, yh], wo[:, cols_ch]).astype(BF).reshape(wide)
         ro.give_core(ch)
-        return carry
-
-    lax.fori_loop(0, CHUNKS, project_out, 0)
-    ro.add_core()
+
+    ro.run(project_out)
     gg.on_far()
     for k in range(1, 8):
         tiny.arrived(k - 1, gc.at[(dp + 8 - k) % 8, yl, z, c, :, 0:CUT], core_dev)
     ggc.start_ring()
     ggc.start_pair()
-    ro.start()
     gat.on_pair()
     gg.done(other_core(gs))
+
+    acc[...] = jnp.zeros_like(acc)
+
+    def back_out(ch, carry):
+        cols_ch = pl.ds(pl.multiple_of(ch * CHUNK, CHUNK), CHUNK)
+        acc[...] += dot_nt(gs[ch].reshape(SEQ, CHUNK), wo[:, cols_ch])
+        return carry
+
+    lax.fori_loop(0, CHUNKS, back_out, 0)
     for ch in range(CHUNKS):
         ms[ch] = gs[ch, :, :, c, :, CUT:]
     for k in range(1, 8):
         to = (dp + k) % 8
         far_cols.start(k - 1, ms.at[to], gc.at[dp, :, :, c, :, CUT:], (to, head))
     gc[dp, :, :, :, :, CUT:] = gs[dp, :, :, :, :, CUT:]
-    lax.fori_loop(1, 8, collect, 0)
-
-    acc[...] = jnp.zeros_like(acc)
-
-    def back_out(ch, carry):
-        cols_ch = pl.ds(pl.multiple_of(ch * CHUNK, CHUNK), CHUNK)
-        acc[...] += dot_nt(gs[ch].reshape(SEQ, CHUNK), wo[:, cols_ch])
-        return carry
-
-    lax.fori_loop(0, CHUNKS, back_out, 0)
     gat.on_ring_own()
     ggc.on_pair()
     key_sum = jnp.zeros((SEQ, HD), F32)
@@ -500,17 +503,14 @@
     gg.sent()
     tiny.sent()
 
-    def back_in(ch, carry):
+    def back_in(ch):
         rows = pl.ds(pl.multiple_of(ch * CHUNK, CHUNK), CHUNK)
         part = dot_nt(qkv[x, yh, :, : HEADS * HD], wq[rows, :])
         part += dot(qkv[x, yh, :, HEADS * HD :], wkv[:, rows])
         gs[ch] = part.astype(BF).reshape(wide)
         rg.give_core(ch)
-        return carry
-
-    lax.fori_loop(0, CHUNKS, back_in, 0)
-    rg.add_core()
-    rg.start()
+
+    rg.run(back_in)
 
     gain_slot = yl * 2 + c
     for ch in range(CHUNKS):
@@ -533,6 +533,8 @@
     gat.on_far()
     rg.middle()
     ggc.on_ring_pair()
+    nc[dp] = xs[dp]
+    lax.fori_loop(1, 8, collect, 0)
     for h in range(2):
         ro.arrived(h)
         for ch in range(4 * h, 4 * h + 4):
@@ -550,22 +552,28 @@
         ga_link.start(5 + k, ga2.at[dp], ga2.at[dp], ((dp + k) % 8, head))
 
     lax.fori_loop(1, 8, collected, 0)
+    early = [(a, b) for a in (x, gqk.prv, gqk.nxt) for b in (yh, 1 - yh)]
+    late = [(gqk.far, yh), (gqk.far, 1 - yh)]
     rg.to_pair()
-    gqk.on_far()
-    total = None
-    for s in range(8):
-        term = dot_tn(nc[s].reshape(SEQ, CHUNK), qkv[s // 2, s % 2])
-        total = term if total is None else total + term
-    gwq_ref[...] = total[:, : HEADS * HD].astype(BF)
-    pairs = total[:, HEADS * HD :].T
-    gwk_ref[...] = pairs[: HD // 2].astype(BF)
-    gwv_ref[...] = pairs[HD // 2 :].astype(BF)
     ggc.on_far()
     for k in range(1, 8):
         ga_link.arrived(5 + k, ga2.at[(dp + 8 - k) % 8], core_dev)
     total = ((ga2[0] + ga2[1]) + (ga2[2] + ga2[3])) + ((ga2[4] + ga2[5]) + (ga2[6] + ga2[7]))
     for ch in range(CHUNKS):
         ggain_ref[:, ch * CHUNK : (ch + 1) * CHUNK] = total[ch : ch + 1]
+    ggc.done(other_core(near_cols))
+    for k in range(1, 8):
+        far_cols.arrived(6 + k, gc.at[(dp + 8 - k) % 8, :, :, 1 - c, :, CUT:], core_dev)
+    total = None
+    for s in range(8):
+        term = dot_tn(att[s // 2, s % 2], gc[s].reshape(SEQ, CHUNK))
+        total = term if total is None else total + term
+    gwo_ref[...] = total.astype(BF)
+
+    total = None
+    for a, b in early:
+        term = dot_tn(nc[2 * a + b].reshape(SEQ, CHUNK), qkv[a, b])
+        total = term if total is None else total + term
     mean = jnp.zeros((ROWS, 1), F32)
     for h in range(2):
         rg.arrived(h)
@@ -579,15 +587,13 @@
         part = inputs_ref[:, span].astype(F32)
         scaled = rg.chunk(ch) * gain_ref[:, span]
         gin_ref[:, span] = (gout_ref[:, span].astype(F32) + inverse_rms * scaled - part * mean).astype(BF)
-    ggc.done(other_core(near_cols))
-    for k in range(1, 8):
-        far_cols.arrived(6 + k, gc.at[(dp + 8 - k) % 8, :, :, 1 - c, :, CUT:], core_dev)
-    total = None
-    for s in range(8):
-        term = dot_tn(att[s // 2, s % 2], gc[s].reshape(SEQ, CHUNK))
-        total = term if total is None else total + term
-    gwo_ref[...] = total.astype(BF)
-
+    gqk.on_far()
+    for a, b in late:
+        total += dot_tn(nc[2 * a + b].reshape(SEQ, CHUNK), qkv[a, b])
+    gwq_ref[...] = total[:, : HEADS * HD].astype(BF)
+    pairs = total[:, HEADS * HD :].T
+    gwk_ref[...] = pairs[: HD // 2].astype(BF)
+    gwv_ref[...] = pairs[HD // 2 :].astype(BF)
     lax.fori_loop(1, 8, spread_sent, 0)
     for link in (gx, gat, gqk, ggc, far_cols, ro, rg, kv_link, ga_link):
         link.sent()
@@ -659,7 +665,7 @@
             pltpu.VMEM((8, CHUNKS, CHUNK), F32),
         ]
         + dma(17) * 2
-        + dma(63)
+        + dma(14)
         + dma(17)
         + dma(14)
         + dma(9) * 2

time: 122 us -> 113 us (0.926)
  Pallas kernels: 121 us -> 112 us
    pallas_call x1, Pallas kernels: 118 us -> 109 us  [per_device(): pl.pallas_call(layer, out_shape=(jax.ShapeDtypeStruct((ROWS, CHUNKS * CHU...]
where the time goes in v5:
time: 113 us
  Pallas kernels  112 us (99%)
    pallas_call x1, Pallas kernels, per_device(): pl.pallas_call(layer, out_shape=(jax.ShapeDtypeStruct((ROWS, CHUNKS * CHU...  109 us
    pallas_call x1, Pallas kernels, per_device(): pl.pallas_call(hand_over, out_shape=[jax.ShapeDtypeStruct(o.shape, o.dtyp...  2.94 us

profile of v5, /device:TPU:1, one launch (start us, length us, event | category | flops | bytes accessed | tf_op | source)
XLA Modules:
  0.0 112.5 jit_solution(6677210402299506382)
XLA Ops:
  0.6 108.8 %shard_map.135 = (bf16[16,8192]{1,0:T(8,128)(2,1)}, bf16[16,8192]{1,0:T(8,128)(2,1)}, f32[1,8192]{1,0:T(1,128)}, bf16[1024,512]{1,0:T(8,128)(2,1)}, bf16[64,1024...) custom-call(bf16[16,8192]{1,0:T(8,128)(2,1)} %inputs_ref.1, f32[1,8192]{1,0:T(1,128)} %bitcast.8, ...), custom_call_target="tpu_custom_call" | custom-call | tf_op jit(solution)/shard_map/pallas_call | solution.py:629
  109.4 2.9 %shard_map.136 = (bf16[16,8192]{1,0:T(8,128)(2,1)}, bf16[16,8192]{1,0:T(8,128)(2,1)}, f32[1,8192]{1,0:T(1,128)}, bf16[1024,512]{1,0:T(8,128)(2,1)}, bf16[64,1024...) custom-call(bf16[16,8192]{1,0:T(8,128)(2,1)} %get-tuple-element.21.refs_0_, ...), custom_call_target="tpu_custom_call" | custom-call | tf_op jit(solution)/shard_map/pallas_call | solution.py:690

commit v6 on v5

--- a/solution.py
+++ b/solution.py
@@ -259,12 +259,13 @@
 
 def layer(
     inputs_ref, gain_ref, doc_ref, wq_hbm, wk_hbm, wv_hbm, wo_hbm, gout_ref,
+    out_hbm, gin_hbm, ggain_hbm, gwq_hbm, gwk_hbm, gwv_hbm, gwo_hbm,
     out_ref, gin_ref, ggain_ref, gwq_ref, gwk_ref, gwv_ref, gwo_ref,
     xs, gs, nc, gc, po, ms, wq, wkv, wo, att, qkv, acc, kvh, kvg, qh, probs,
     rs0, rs1, rs2, rs3, rs4, rs5, rt1, rt2, rt3, rt4, rt5,
     ga0, ga1, ga2,
     x_s, x_r, g_s, g_r, nc_s, nc_r, gc_s, gc_r, fc_s, fc_r, at_s, at_r, qk_s, qk_r, ro_s, ro_r, rg_s, rg_r,
-    tn_s, tn_r, kv_s, kv_r, ga_s, ga_r, w_sem,
+    tn_s, tn_r, kv_s, kv_r, ga_s, ga_r, w_sem, o_sem,
 ):
     dp, head = lax.axis_index("dp"), lax.axis_index("head")
     x, yh = dp // 2, dp % 2
@@ -286,6 +287,15 @@
     for cp in weights:
         cp.start()
 
+    results = [
+        pltpu.make_async_copy(out_ref, out_hbm, o_sem.at[0]),
+        pltpu.make_async_copy(gin_ref, gin_hbm, o_sem.at[1]),
+        pltpu.make_async_copy(ggain_ref, ggain_hbm, o_sem.at[2]),
+        pltpu.make_async_copy(gwq_ref, gwq_hbm, o_sem.at[3]),
+        pltpu.make_async_copy(gwk_ref, gwk_hbm, o_sem.at[4]),
+        pltpu.make_async_copy(gwv_ref, gwv_hbm, o_sem.at[5]),
+        pltpu.make_async_copy(gwo_ref, gwo_hbm, o_sem.at[6]),
+    ]
     barrier = pltpu.get_barrier_semaphore()
     partners = [core_dev, pair_dev, diag_dev] + z_dev[1:] + dp_devs
     for to in partners:
@@ -540,6 +550,7 @@
         for ch in range(4 * h, 4 * h + 4):
             span = slice(ch * CHUNK, (ch + 1) * CHUNK)
             out_ref[:, span] = (inputs_ref[:, span].astype(F32) + ro.chunk(ch)).astype(BF)
+    results[0].start()
     gqk.on_ring_pair()
     for k in range(1, 8):
         block = gc.at[(dp + 8 - k) % 8, :, :, c, :, CUT:]
@@ -561,6 +572,7 @@
     total = ((ga2[0] + ga2[1]) + (ga2[2] + ga2[3])) + ((ga2[4] + ga2[5]) + (ga2[6] + ga2[7]))
     for ch in range(CHUNKS):
         ggain_ref[:, ch * CHUNK : (ch + 1) * CHUNK] = total[ch : ch + 1]
+    results[2].start()
     ggc.done(other_core(near_cols))
     for k in range(1, 8):
         far_cols.arrived(6 + k, gc.at[(dp + 8 - k) % 8, :, :, 1 - c, :, CUT:], core_dev)
@@ -569,6 +581,7 @@
         term = dot_tn(att[s // 2, s % 2], gc[s].reshape(SEQ, CHUNK))
         total = term if total is None else total + term
     gwo_ref[...] = total.astype(BF)
+    results[6].start()
 
     total = None
     for a, b in early:
@@ -587,22 +600,39 @@
         part = inputs_ref[:, span].astype(F32)
         scaled = rg.chunk(ch) * gain_ref[:, span]
         gin_ref[:, span] = (gout_ref[:, span].astype(F32) + inverse_rms * scaled - part * mean).astype(BF)
+    results[1].start()
     gqk.on_far()
     for a, b in late:
         total += dot_tn(nc[2 * a + b].reshape(SEQ, CHUNK), qkv[a, b])
     gwq_ref[...] = total[:, : HEADS * HD].astype(BF)
+    results[3].start()
     pairs = total[:, HEADS * HD :].T
     gwk_ref[...] = pairs[: HD // 2].astype(BF)
     gwv_ref[...] = pairs[HD // 2 :].astype(BF)
+    results[4].start()
+    results[5].start()
     lax.fori_loop(1, 8, spread_sent, 0)
     for link in (gx, gat, gqk, ggc, far_cols, ro, rg, kv_link, ga_link):
         link.sent()
+    for cp in results:
+        cp.wait()
 
 
 def hand_over(*refs):
     src, dst, mid, sem_in, sem_out = refs[:7], refs[7:14], refs[14:21], refs[21], refs[22]
-    loads = [pltpu.make_async_copy(src[i], mid[i], sem_in.at[i]) for i in range(7)]
-    stores = [pltpu.make_async_copy(mid[i], dst[i], sem_out.at[i]) for i in range(7)]
+    parts = []
+    for i in (3, 6, 0, 1, 4, 5, 2):
+        rows = src[i].shape[0]
+        step = rows // 2 if rows >= 256 else rows
+        parts += [(i, slice(low, low + step)) for low in range(0, rows, step)]
+    loads = [
+        pltpu.make_async_copy(src[i].at[rows], mid[i].at[rows], sem_in.at[n])
+        for n, (i, rows) in enumerate(parts)
+    ]
+    stores = [
+        pltpu.make_async_copy(mid[i].at[rows], dst[i].at[rows], sem_out.at[n])
+        for n, (i, rows) in enumerate(parts)
+    ]
     for cp in loads:
         cp.start()
     for load, store in zip(loads, stores):
@@ -626,20 +656,22 @@
         pltpu.VMEM((CHUNKS, ROWS, CHUNK), BF),
     ]
     dma = lambda n: [pltpu.SemaphoreType.DMA((n,))] * 2
+    results = (
+        jax.ShapeDtypeStruct((ROWS, CHUNKS * CHUNK), BF),
+        jax.ShapeDtypeStruct((ROWS, CHUNKS * CHUNK), BF),
+        jax.ShapeDtypeStruct((1, CHUNKS * CHUNK), F32),
+        jax.ShapeDtypeStruct((CHUNK, HEADS * HD), BF),
+        jax.ShapeDtypeStruct((HD // 2, CHUNK), BF),
+        jax.ShapeDtypeStruct((HD // 2, CHUNK), BF),
+        jax.ShapeDtypeStruct((HEADS * HD, CHUNK), BF),
+    )
     outs = pl.pallas_call(
         layer,
-        out_shape=(
-            jax.ShapeDtypeStruct((ROWS, CHUNKS * CHUNK), BF),
-            jax.ShapeDtypeStruct((ROWS, CHUNKS * CHUNK), BF),
-            jax.ShapeDtypeStruct((1, CHUNKS * CHUNK), F32),
-            jax.ShapeDtypeStruct((CHUNK, HEADS * HD), BF),
-            jax.ShapeDtypeStruct((HD // 2, CHUNK), BF),
-            jax.ShapeDtypeStruct((HD // 2, CHUNK), BF),
-            jax.ShapeDtypeStruct((HEADS * HD, CHUNK), BF),
-        ),
+        out_shape=results,
         in_specs=[vmem] * 3 + [hbm] * 4 + [vmem],
-        out_specs=[vmem] * 7,
-        scratch_shapes=[
+        out_specs=[hbm] * 7,
+        scratch_shapes=[pltpu.VMEM(o.shape, o.dtype) for o in results]
+        + [
             pltpu.VMEM(rows, BF),
             pltpu.VMEM(rows, BF),
             pltpu.VMEM(rows, BF),
@@ -673,7 +705,7 @@
         + dma(7)
         + dma(2)
         + dma(13)
-        + [pltpu.SemaphoreType.DMA((4,))],
+        + [pltpu.SemaphoreType.DMA((4,)), pltpu.SemaphoreType.DMA((7,))],
         compiler_params=pltpu.CompilerParams(
             collective_id=0, has_side_effects=True, vmem_limit_bytes=62 * 2**20
         ),
@@ -692,7 +724,7 @@
         out_shape=[jax.ShapeDtypeStruct(o.shape, o.dtype) for o in outs],
         in_specs=[hbm] * 7,
         out_specs=[hbm] * 7,
-        scratch_shapes=[pltpu.VMEM(o.shape, o.dtype) for o in outs] + dma(7),
+        scratch_shapes=[pltpu.VMEM(o.shape, o.dtype) for o in outs] + dma(9),
     )(*outs)
     return (out, gin, ggain.reshape(-1), gwq, gwk.T, gwv.T, gwo)
 

time: 113 us -> 112 us (level)
  no operation moved by 1% of the time
where the time goes in v6:
time: 112 us; the launch traced here: 111 us
  Pallas kernels  111 us (99%)
    pallas_call x1, Pallas kernels, per_device(): pl.pallas_call(layer, out_shape=results, in_specs=[vmem] * 3 + [hbm] * 4...  108 us
    pallas_call x1, Pallas kernels, per_device(): pl.pallas_call(hand_over, out_shape=[jax.ShapeDtypeStruct(o.shape, o.dtyp...  2.76 us

profile of v6, /device:TPU:1, one launch (start us, length us, event | category | flops | bytes accessed | tf_op | source)
XLA Modules:
  0.0 111.4 jit_solution(1235354315824256708)
XLA Ops:
  0.6 107.8 %shard_map.135 = (bf16[16,8192]{1,0:T(8,128)(2,1)}, bf16[16,8192]{1,0:T(8,128)(2,1)}, f32[1,8192]{1,0:T(1,128)}, bf16[1024,512]{1,0:T(8,128)(2,1)}, bf16[64,1024...) custom-call(bf16[16,8192]{1,0:T(8,128)(2,1)} %inputs_ref.1, f32[1,8192]{1,0:T(1,128)} %bitcast.8, ...), custom_call_target="tpu_custom_call" | custom-call | tf_op jit(solution)/shard_map/pallas_call | solution.py:668
  108.4 2.8 %shard_map.136 = (bf16[16,8192]{1,0:T(8,128)(2,1)}, bf16[16,8192]{1,0:T(8,128)(2,1)}, f32[1,8192]{1,0:T(1,128)}, bf16[1024,512]{1,0:T(8,128)(2,1)}, bf16[64,1024...) custom-call(bf16[16,8192]{1,0:T(8,128)(2,1)} %get-tuple-element.21.refs_0_, ...), custom_call_target="tpu_custom_call" | custom-call | tf_op jit(solution)/shard_map/pallas_call | solution.py:722
